TPU v7x, 512 devices: a whole 4x4x16 slice. The times are simulated.
512 devices in a mesh: ctx: 32 (over z_lo, y), grp: 16 (over x, z_hi, core).
Axes of the slice: x: 4, y: 4, z: 16 (z_hi: 2, z_lo: 8; z = z_hi * 8 + z_lo), core: 2. Of those that a mesh axis runs over, the one named last changes fastest.
Arguments:
- q_nope: bfloat16 [256, 128, 128], P(None, 'ctx'), may hold values from -6 to 6
- q_rope: bfloat16 [256, 128, 64], P(None, 'ctx'), may hold values from -720 to 720
- w_uk: bfloat16 [128, 128, 512], P('ctx'), may hold values from -0.5 to 0.5
- w_uv: bfloat16 [128, 512, 128], P('ctx'), may hold values from -0.375 to 0.375
- prompt: bfloat16 [6144, 576], P('grp'), may hold values from -12 to 12
- w_out: bfloat16 [16384, 7168], P('ctx', 'grp'), may hold values from -0.0625 to 0.0625
- residual: bfloat16 [256, 7168], P('ctx', 'grp'), may hold values from -3 to 3
- routes: int32 [256, 8], P('ctx'), may hold values from 0 to 31, all different within a row; in each aligned block of 8 rows (0 to 7, 8 to 15, ...) at most 4 rows name the same one
- route_scores: float32 [256, 8], P('ctx'), may hold values from 0.05 to 1
- expert_gate: bfloat16 [32, 7168, 1024], P('ctx', 'grp'), may hold values from -0.0625 to 0.0625
- expert_up: bfloat16 [32, 7168, 1024], P('ctx', 'grp'), may hold values from -0.0625 to 0.0625
- expert_down: bfloat16 [32, 1024, 7168], P('ctx', None, 'grp'), may hold values from -0.1875 to 0.1875
Outputs:
- layer_out: bfloat16 [256, 7168], P('ctx', 'grp')
Inputs may be any that keep to these rules, and one draw needn't show every extreme that they name: `routes`: in each aligned block of 8 rows no expert is named by more than 4 rows, a bound that some block reaches; the 8 experts of a row differ.
All inputs are finite; a program needn't handle non-finite values.
Results may differ from a plain program's by a relative error of at most 0.0163.
Values may be sent and summed in bfloat16 or wider, within the bound.
A program may use at most 64 MiB of HBM per device.

v0:
```python
import jax
import jax.numpy as jnp
from jax import lax
from jax.sharding import PartitionSpec as P

NOPE = 128
ROPE = 64
LAT = 512
VDIM = 128
CAP = 4


route_factor = 2.5


def per_device(
    q_nope,
    q_rope,
    w_uk,
    w_uv,
    prompt,
    w_out,
    residual,
    routes,
    route_scores,
    expert_gate,
    expert_up,
    expert_down,
):
    score_scale = (NOPE + ROPE) ** (-0.5)
    q_latent = jnp.einsum("rhn,hnl->rhl", q_nope, w_uk, preferred_element_type=jnp.float32).astype(
        jnp.bfloat16
    )
    queries = jnp.concatenate([q_latent, q_rope], axis=-1)
    head_uv = w_uv.astype(jnp.float32)
    head_cols = queries.shape[1] * VDIM
    all_keys = lax.all_gather(prompt, "grp", axis=0, tiled=True)
    row_share = queries.shape[0] // lax.axis_size("grp")
    own_queries = lax.dynamic_slice_in_dim(queries, lax.axis_index("grp") * row_share, row_share, 0)
    scores = (
        jnp.einsum("rhc,jc->rhj", own_queries, all_keys, preferred_element_type=jnp.float32)
        * score_scale
    )
    top_score = jnp.max(scores, axis=-1)
    raised = jnp.exp(scores - top_score[..., None])
    denominator = jnp.sum(raised, axis=-1)
    weighted = jnp.einsum(
        "rhj,jl->rhl",
        raised.astype(jnp.bfloat16),
        all_keys[:, :LAT],
        preferred_element_type=jnp.float32,
    )
    values = jnp.einsum("rhl,hlv->rhv", weighted, head_uv, precision=lax.Precision.HIGHEST)
    top_score, denominator, values = (top_score, denominator, values)
    own_rows = (values / denominator[..., None]).astype(jnp.bfloat16).reshape(row_share, head_cols)
    attended = lax.all_gather(own_rows, "grp", axis=0, tiled=True)
    local_rows = residual.shape[0]
    projected = lax.psum_scatter(
        jnp.dot(attended, w_out, preferred_element_type=jnp.float32),
        "ctx",
        scatter_dimension=0,
        tiled=True,
    )
    hidden = residual.astype(jnp.float32) + projected
    moe_input = hidden.astype(jnp.bfloat16)
    gate_weights = route_factor * route_scores / jnp.sum(route_scores, axis=-1, keepdims=True)
    top_count = routes.shape[1]
    experts = expert_gate.shape[0] * lax.axis_size("ctx")
    flat_routes = routes.reshape(-1)
    onehot = (flat_routes[:, None] == jnp.arange(experts, dtype=jnp.int32)[None, :]).astype(
        jnp.int32
    )
    before = jnp.cumsum(onehot, axis=0) - onehot
    slot_index = jnp.sum(before * onehot, axis=1)
    target = flat_routes * CAP + slot_index
    select = (target[:, None] == jnp.arange(experts * CAP, dtype=jnp.int32)[None, :]).astype(
        jnp.float32
    )
    row_of = jnp.arange(local_rows * top_count, dtype=jnp.int32) // top_count
    row_pick = (row_of[:, None] == jnp.arange(local_rows, dtype=jnp.int32)[None, :]).astype(
        jnp.float32
    )
    slot_rows = jnp.dot(select.T, row_pick, precision=lax.Precision.HIGHEST)
    outgoing = jnp.dot(
        slot_rows.astype(jnp.bfloat16), moe_input, preferred_element_type=jnp.float32
    ).astype(jnp.bfloat16)
    outgoing = outgoing.reshape(experts, 1, CAP, moe_input.shape[1])
    slot_weights = jnp.dot(
        row_pick.T, select * gate_weights.reshape(-1)[:, None], precision=lax.Precision.HIGHEST
    )
    arrived = lax.all_to_all(outgoing, "ctx", split_axis=0, concat_axis=1, tiled=True)
    gate_part = jnp.einsum(
        "escd,edf->escf", arrived, expert_gate, preferred_element_type=jnp.float32
    )
    up_part = jnp.einsum("escd,edf->escf", arrived, expert_up, preferred_element_type=jnp.float32)
    gate_sum, up_sum = lax.psum((gate_part, up_part), "grp")
    activated = (jax.nn.silu(gate_sum) * up_sum).astype(jnp.bfloat16)
    result = jnp.einsum(
        "escf,efd->escd", activated, expert_down, preferred_element_type=jnp.float32
    ).astype(jnp.bfloat16)
    returned = lax.all_to_all(result, "ctx", split_axis=1, concat_axis=0, tiled=True)
    returned = returned.reshape(experts * CAP, moe_input.shape[1]).astype(jnp.float32)
    combined = jnp.dot(slot_weights, returned, precision=lax.Precision.HIGHEST)
    return (hidden + combined).astype(jnp.bfloat16)


def solution(mesh):
    in_specs = (
        P(None, "ctx", None),
        P(None, "ctx", None),
        P("ctx", None, None),
        P("ctx", None, None),
        P("grp", None),
        P("ctx", "grp"),
        P("ctx", "grp"),
        P("ctx", None),
        P("ctx", None),
        P("ctx", "grp", None),
        P("ctx", "grp", None),
        P("ctx", None, "grp"),
    )
    out_specs = P("ctx", "grp")
    return jax.shard_map(
        per_device, mesh=mesh, in_specs=in_specs, out_specs=out_specs, check_vma=False
    )
```

profile of v0, /device:TPU:1, one launch (start us, length us, event | category | flops | bytes accessed | tf_op | source)
XLA Modules:
  0.0 790.0 jit_solution(4318295882476667328)
XLA Ops:
  6.5 0.7 all-gather.2.cloned.1.call-update
  7.3 1.6 fusion.8
  8.9 172.9 %all-gather.2.cloned.1.call-done = bf16[6144,576]{0,1:T(8,128)(2,1)} async-done(((bf16[384,576]{0,1:T(8,128)(2,1)}), bf16[6144,576]{0,1:T(8,128)(2,1)}) %all-gather.2.cloned.1.call-update) | async-done | bytes 7077904 | tf_op jit(solution)/shard_map/all_gather | solution.py:37
  181.8 4.4 fusion.42
  186.2 0.4 fusion.6
  186.5 0.3 copy-done.1
  186.9 2.0 fusion.5
  189.0 0.3 fusion.12
  189.3 35.4 %all_gather.7 = bf16[256,512]{1,0:T(8,128)(2,1)S(1)} all-gather(bf16[16,512]{1,0:T(8,128)(2,1)S(1)} %bitcast.63), channel_id=1, replica_groups=mesh['ctx'=32,'grp'=16] {'grp'}, dimensions={0}, use_global_device_ids=true | all-gather | bytes 278528 | tf_op jit(solution)/shard_map/all_gather | solution.py:56
  224.7 1.1 fusion.43
  225.9 0.1 reshape.68
  226.0 0.1 fusion.29
  226.0 0.1 reduce_window_sum.11
  226.1 0.2 select_reduce_fusion
  226.3 0.3 convolution_convert_fusion.3
  226.6 210.9 %reduce-scatter.2.cloned.1.call-done = f32[8,448]{1,0:T(8,128)} async-done(((f32[256,448]{1,0:T(8,128)}), f32[8,448]{1,0:T(8,128)}) %reduce-scatter.2.cloned.1.call-update) | async-done | bytes 14352 | tf_op jit(solution)/shard_map/reduce_scatter | solution.py:58
  437.5 1.0 convolution_convert_fusion.2
  438.5 0.1 copy.25
  438.7 15.1 %all_to_all.8 = bf16[32,1,4,448]{3,2,1,0:T(4,128)(2,1)S(1)} all-to-all(bf16[32,1,4,448]{3,2,1,0:T(4,128)(2,1)S(1)} %bitcast.62), channel_id=1, replica_groups=mesh['ctx'=32,'grp'=16] {'ctx'}, dimensions={0} | all-to-all | bytes 229376 | tf_op jit(solution)/shard_map/all_to_all | solution.py:91
  453.7 1.1 convolution_bitcast_fusion
  454.9 1.1 convolution_bitcast_fusion.1
  456.0 0.1 reduce_sum.29
  456.1 307.4 %all-reduce.3.cloned.1.call-done = (f32[1,32,4,1024]{3,1,2,0:T(8,128)}, f32[1,32,4,1024]{3,1,2,0:T(8,128)}) async-done(((f32[1,32,4,1024]{3,1,2,0:T(8,128)}, f32[1,32,4,1024]{3,1,2,0:T(8,128)}), (f32[1,32,4,1024]{3,1,2,0:T(8,128)}, f32[1,32,4,1024]{3,1,2,0:T(8,128)})) %all-reduce.3.cloned.1.call-update) | async-done | bytes 1048592 | tf_op jit(solution)/shard_map/psum | solution.py:96
  763.5 1.6 fusion.9
  765.1 0.7 copy.28
  765.9 4.7 all-to-all-start.1
  770.5 0.1 multiply_divide_fusion
  770.6 0.1 mul.53
  770.7 0.3 fusion.27
  771.0 11.7 %all-to-all-done.1 = bf16[1,32,4,448]{3,2,0,1:T(4,128)(2,1)S(1)} async-done(((bf16[1,32,4,448]{3,2,0,1:T(4,128)(2,1)}), bf16[1,32,4,448]{3,2,0,1:T(4,128)(2,1)S(1)}, u32[]{:S(2)}, u32[]{:S(2)}) %all-to-all-start.1) | async-done | bytes 114720 | tf_op jit(solution)/shard_map/all_to_all | solution.py:101
  782.7 0.1 reshape.75
  782.7 0.8 fusion.13
  (29 shorter events, 0.2 us)
Async XLA Ops:
  6.5 447.2 %copy-start = (bf16[1,448,1024]{2,1,0:T(8,128)(2,1)S(1)}, bf16[1,448,1024]{2,1,0:T(8,128)(2,1)}, u32[]{:S(2)}) copy-start(bf16[1,448,1024]{2,1,0:T(8,128)(2,1)} %param.22) | copy-start | bytes 2752516
  6.5 175.3 %copy-start.5 = (bf16[256,4,64]{0,2,1:T(8,128)(2,1)S(1)}, bf16[256,4,64]{0,2,1:T(8,128)(2,1)}, u32[]{:S(2)}) copy-start(bf16[256,4,64]{0,2,1:T(8,128)(2,1)} %param.13) | copy-start | bytes 393220
  6.5 175.3 %all-gather.2.cloned.1.call-start = ((), (), s32[]{:S(2)}) async-start(), calls=%async_computation.3 | async-start | bytes 7520256 | tf_op jit(solution)/shard_map/all_gather | solution.py:37
  7.3 430.2 %reduce-scatter.2.cloned.1.call-start = ((), (), s32[]{:S(2)}) async-start(), calls=%async_computation.4 | async-start | bytes 540672 | tf_op jit(solution)/shard_map/reduce_scatter | solution.py:58
  181.8 5.1 copy-start.1
  186.9 2.0 copy-start.3
  186.9 37.8 %copy-start.4 = (bf16[512,448]{0,1:T(8,128)(2,1)S(1)}, bf16[512,448]{0,1:T(8,128)(2,1)}, u32[]{:S(2)}) copy-start(bf16[512,448]{0,1:T(8,128)(2,1)} %param.17) | copy-start | bytes 1376260
  188.9 36.9 %copy-start.9 = (s32[8,8]{1,0:T(8,128)S(1)}, s32[8,8]{1,0:T(8,128)}, u32[]{:S(2)}) copy-start(s32[8,8]{1,0:T(8,128)} %param.19) | copy-start | bytes 772
  188.9 248.6 %copy-start.7 = (bf16[8,448]{1,0:T(8,128)(2,1)S(1)}, bf16[8,448]{1,0:T(8,128)(2,1)}, u32[]{:S(2)}) copy-start(bf16[8,448]{1,0:T(8,128)(2,1)} %param.18) | copy-start | bytes 21508
  225.8 229.1 %copy-start.2 = (bf16[1,448,1024]{2,1,0:T(8,128)(2,1)S(1)}, bf16[1,448,1024]{2,1,0:T(8,128)(2,1)}, u32[]{:S(2)}) copy-start(bf16[1,448,1024]{2,1,0:T(8,128)(2,1)} %param.21) | copy-start | bytes 2752516
  225.8 537.6 %all-reduce.3.cloned.1.call-start = ((), (), s32[]{:S(2)}) async-start(), calls=%async_computation.5 | async-start | bytes 2097152 | tf_op jit(solution)/shard_map/psum | solution.py:96
  454.9 1.1 copy-start.8
  454.9 308.6 %copy-start.10 = (bf16[1,1024,448]{1,2,0:T(8,128)(2,1)S(1)}, bf16[1,1024,448]{1,2,0:T(8,128)(2,1)}, u32[]{:S(2)}) copy-start(bf16[1,1024,448]{1,2,0:T(8,128)(2,1)} %param.23) | copy-start | bytes 2752516
  763.5 19.3 %copy-start.6 = (f32[8,448]{1,0:T(8,128)S(1)}, f32[8,448]{1,0:T(8,128)}, u32[]{:S(2)}) copy-start(f32[8,448]{1,0:T(8,128)} %reduce-scatter.2.cloned.1.call-done) | copy-start | bytes 43012
  765.9 16.8 %all-to-all-start.1 = ((bf16[1,32,4,448]{3,2,0,1:T(4,128)(2,1)}), bf16[1,32,4,448]{3,2,0,1:T(4,128)(2,1)S(1)}, u32[]{:S(2)}, u32[]{:S(2)}) async-start(bf16[1,32,4,448]{3,2,0,1:T(4,128)(2,1)} %copy.28), calls=%async_computation.2 | async-start | bytes 262144 | tf_op jit(solution)/shard_map/all_to_all | solution.py:101
Sparse Core Ops, SparseCore 0:
  10.5 171.2 all-gather.1
  225.9 211.5 reduce-scatter.1
  456.1 307.3 all-reduce.2
where the time goes:
time: 794 us; the launch traced here: 790 us
  waiting for transfers between devices  704 us (89%)
  blocking collectives  50.5 us (6%)
  matrix products  15.5 us (2%)
  between operations  13.2 us (2%)
    psum x1, waiting for transfers between devices, per_device(): gate_sum, up_sum = lax.psum((gate_part, up_part), 'grp')  307 us
    reduce_scatter x1, waiting for transfers between devices, per_device(): lax.psum_scatter(jnp.dot(attended, w_out, preferred_element_type=jnp.floa...  211 us
    all_gather x1, waiting for transfers between devices, per_device(): all_keys = lax.all_gather(prompt, 'grp', axis=0, tiled=True)  173 us
    all_gather x1, blocking collectives, per_device(): attended = lax.all_gather(own_rows, 'grp', axis=0, tiled=True)  35.4 us
  transfers between devices with their start and end apart: 4, of which 4 were waited for; matrix products, arithmetic and copies ran while one was open for 0% of the time, Pallas kernels for 0%

commit v1 on v0

v1 whole, which is shorter than its diff:
```python
import jax
import jax.numpy as jnp
from jax import lax
from jax.experimental import pallas as pl
from jax.experimental.pallas import tpu as pltpu
from jax.sharding import PartitionSpec as P

NOPE = 128
ROPE = 64
LAT = 512
VDIM = 128
CAP = 4
TOPK = 8
FF = 1024
ROWS = 256
HEADS = 4
KEYS = 384
COLS = 448
LANES = 128
PAD = 512
QS = PAD // LANES
ROW_DEV = 8
NZ, NY, NX = 8, 4, 4
NCTX = NZ * NY
SLOTS = NCTX * CAP
ROUTE_FACTOR = 2.5
FAR_FIRST = (2, 1, 3, 0)
F32 = jnp.float32
BF16 = jnp.bfloat16
MESH = pl.DeviceIdType.MESH


def dot(a, b, ca, cb):
    return lax.dot_general(a, b, (((ca,), (cb,)), ((), ())), preferred_element_type=F32)


def split(a):
    high = a.astype(BF16)
    return high, (a - high.astype(F32)).astype(BF16)


def kernel(
    qn, qr, w_uk, w_uv, prompt, residual, routes, scores, w_out_hbm, wg_hbm, wu_hbm, wd_hbm,
    out,
    w_out, wgu, wd, perm, perm_t,
    obuf, lse, o_recv, l_recv, zh_send, zh_recv, zl_send, zl_recv, att,
    proj, pbuf, p_recv, zbuf, z_recv, res_pad, disp, arrived,
    gu, gu_recv, gz_send, gz_recv, act, down, ret, ret_recv,
    load_sem, o_sem, l_sem, zh_sem, ag_sem, y_sem, z_sem, d_sem, g_sem, gz_sem, act_sem, r_sem,
):
    me_c = lax.axis_index("ctx")
    me_g = lax.axis_index("grp")
    z, y = me_c // NY, me_c % NY
    x, zh, core = me_g // 4, (me_g // 2) % 2, me_g % 2
    me_q = x * 2 + core
    partner = {"grp": x * 4 + (1 - zh) * 2 + core}

    def near(d, c):
        return {"grp": ((x + d) % NX) * 4 + zh * 2 + c}

    barrier = pltpu.get_barrier_semaphore()
    for d in range(NX):
        if d:
            for c in range(2):
                pl.semaphore_signal(barrier, inc=1, device_id=near(d, c), device_id_type=MESH)
    pl.semaphore_signal(barrier, inc=1, device_id=near(0, 1 - core), device_id_type=MESH)
    pl.semaphore_signal(barrier, inc=1, device_id=partner, device_id_type=MESH)

    def greet(d, carry):
        pl.semaphore_signal(
            barrier, inc=1, device_id={"ctx": (me_c + d) % NCTX}, device_id_type=MESH
        )
        return carry

    lax.fori_loop(1, NCTX, greet, 0)

    loads = [
        pltpu.make_async_copy(w_out_hbm, w_out, load_sem.at[0]),
        pltpu.make_async_copy(wg_hbm, wgu.at[pl.ds(0, COLS), pl.ds(0, FF)], load_sem.at[1]),
        pltpu.make_async_copy(wu_hbm, wgu.at[pl.ds(0, COLS), pl.ds(FF, FF)], load_sem.at[2]),
        pltpu.make_async_copy(wd_hbm, wd, load_sem.at[3]),
    ]
    for load in loads:
        load.start()
    sent = []

    def send(src, dst, sems, n, at, device):
        copy = pltpu.make_async_remote_copy(
            src_ref=src, dst_ref=dst, send_sem=sems.at[0, n], recv_sem=sems.at[1, at],
            device_id=device, device_id_type=MESH,
        )
        copy.start()
        sent.append((src, sems, n))

    def arrive(dst, sems, at):
        pltpu.make_async_remote_copy(
            src_ref=dst, dst_ref=dst, send_sem=sems.at[0, at], recv_sem=sems.at[1, at],
            device_id=partner, device_id_type=MESH,
        ).wait_recv()

    scale = (NOPE + ROPE) ** -0.5
    latents = prompt[:, 0:LAT]
    rotated = prompt[:, LAT : LAT + ROPE]
    for step, d in enumerate(FAR_FIRST):
        h = (x + d) % NX
        q_latent = dot(qn[h], w_uk[h], 1, 0).astype(BF16)
        s = (dot(latents, q_latent, 1, 1) + dot(rotated, qr[h], 1, 1)) * scale
        top = jnp.max(s, axis=0, keepdims=True)
        raised = jnp.exp(s - top)
        total = jnp.sum(raised, axis=0, keepdims=True)
        weighted = dot(latents, raised.astype(BF16), 0, 0)
        high, low = split(weighted)
        values = dot(w_uv[h], high, 0, 0) + dot(w_uv[h], low, 0, 0)
        o = (values / total).astype(BF16)
        obuf[h] = o.reshape(2, VDIM // 2, ROWS)
        lse[h] = jnp.broadcast_to(top + jnp.log(total), (8, ROWS))
        if step == 0:
            pl.semaphore_wait(barrier, 2 * NX - 1 + 1 + NCTX - 1)
        for c in range(2) if d else (1 - core,):
            send(obuf.at[h, c], o_recv.at[d * 2 + core], o_sem, d * 2 + c, d * 2 + core, near(d, c))
            send(lse.at[h], l_recv.at[d * 2 + core], l_sem, d * 2 + c, d * 2 + core, near(d, c))
        if d == 0:
            o_recv[core] = obuf[h, core]
            l_recv[core] = lse[h]

    wgu[COLS:PAD, :] = jnp.zeros((PAD - COLS, 2 * FF), BF16)
    slot = lax.broadcasted_iota(jnp.int32, (PAD, PAD), 0)
    place = lax.broadcasted_iota(jnp.int32, (PAD, PAD), 1)

    def place_of(k):
        k2 = k % SLOTS
        return (k2 // CAP) * (QS * CAP) + (k // SLOTS) * CAP + k2 % CAP

    perm[...] = jnp.where(place_of(slot) == place, 1.0, 0.0).astype(BF16)
    perm_t[...] = jnp.where(place_of(place) == slot, 1.0, 0.0).astype(BF16)
    res_pad[...] = jnp.zeros((ROW_DEV, PAD), F32)
    res_pad[:, 0:COLS] = residual[...].astype(F32)
    proj[:, PAD - LANES : PAD] = jnp.zeros((ROWS, LANES), F32)
    down[:, PAD - LANES : PAD] = jnp.zeros((SLOTS, LANES), F32)

    lane = lax.broadcasted_iota(jnp.int32, (ROW_DEV, PAD), 1)
    expert_of = lane // (QS * CAP)
    scored = scores[...]
    gate_weights = ROUTE_FACTOR * scored / jnp.sum(scored, axis=1, keepdims=True)
    chosen = jnp.zeros((ROW_DEV, PAD), F32)
    weight = jnp.zeros((ROW_DEV, PAD), F32)
    for k in range(TOPK):
        hit = routes[:, k : k + 1] == expert_of
        chosen = chosen + jnp.where(hit, 1.0, 0.0)
        weight = weight + jnp.where(hit, gate_weights[:, k : k + 1], 0.0)
    row = lax.broadcasted_iota(jnp.int32, (ROW_DEV, PAD), 0)
    before = jnp.zeros((ROW_DEV, PAD), F32)
    for r in range(ROW_DEV - 1):
        before = before + jnp.where(row > r, chosen[r : r + 1, :], 0.0)
    picked = jnp.where(before == (lane % CAP).astype(F32), chosen, 0.0)
    block_of = (lane // CAP) % QS
    pick = jnp.concatenate([jnp.where(block_of == q, picked, 0.0) for q in range(QS)], axis=0)
    pick_weight = jnp.concatenate(
        [jnp.where(block_of == q, picked * weight, 0.0) for q in range(QS)], axis=0
    )

    for d in FAR_FIRST:
        for c in range(2) if d else (1 - core,):
            arrive(o_recv.at[d * 2 + c], o_sem, d * 2 + c)
            arrive(l_recv.at[d * 2 + c], l_sem, d * 2 + c)

    def merge(outs, sums):
        top = sums[0]
        for v in sums[1:]:
            top = jnp.maximum(top, v)
        scaled = [jnp.exp(v - top) for v in sums]
        total = scaled[0]
        for v in scaled[1:]:
            total = total + v
        o = jnp.zeros(outs[0].shape, F32)
        for v, s in zip(outs, scaled):
            o = o + v.astype(F32) * s
        return o / total, top + jnp.log(total)

    o, l = merge([o_recv[i] for i in range(2 * NX)], [l_recv[i, 0:1, :] for i in range(2 * NX)])
    zh_send[...] = o.astype(BF16)
    zl_send[...] = jnp.broadcast_to(l, (8, ROWS))
    send(zh_send, zh_recv, zh_sem, 0, 0, partner)
    send(zl_send, zl_recv, zh_sem, 1, 1, partner)
    arrive(zh_recv, zh_sem, 0)
    arrive(zl_recv, zh_sem, 1)
    o, _ = merge([zh_send[...], zh_recv[...]], [l, zl_recv[0:1, :]])
    att[me_q] = o.astype(BF16)
    for d in FAR_FIRST:
        for c in range(2) if d else (1 - core,):
            send(att.at[me_q], att.at[me_q], ag_sem, d * 2 + c, d * 2 + core, near(d, c))
    for d in FAR_FIRST:
        for c in range(2) if d else (1 - core,):
            arrive(att.at[((x + NX - d) % NX) * 2 + c], ag_sem, d * 2 + c)

    loads[0].wait()
    proj[:, 0:COLS] = dot(att[...].reshape(HEADS * VDIM, ROWS), w_out[...], 0, 0)
    for to in range(NY):
        parts = []
        for q in range(QS):
            part = proj[:, q * LANES : (q + 1) * LANES].reshape(NZ, NY, ROW_DEV, LANES)
            parts.append(part[:, to])
        pbuf[to] = jnp.stack(parts, axis=1).reshape(NZ * QS * ROW_DEV, LANES).astype(BF16)
    for d in (2, 1, 3):
        to = (y + d) % NY
        send(pbuf.at[to], p_recv.at[d], y_sem, d, d, {"ctx": z * NY + to})
    total = pbuf[y].astype(F32)
    for d in (1, 3, 2):
        arrive(p_recv.at[d], y_sem, d)
        total = total + p_recv[d].astype(F32)
    zbuf[...] = total.reshape(NZ, QS * ROW_DEV, LANES).astype(BF16)
    for d in (4, 3, 5, 2, 6, 1, 7):
        to = (z + d) % NZ
        send(zbuf.at[to], z_recv.at[d], z_sem, d, d, {"ctx": to * NY + y})
    hidden = jnp.concatenate([res_pad[:, q * LANES : (q + 1) * LANES] for q in range(QS)], axis=0)
    hidden = hidden + zbuf[z].astype(F32)
    for d in (1, 7, 2, 6, 3, 5, 4):
        arrive(z_recv.at[d], z_sem, d)
        hidden = hidden + z_recv[d].astype(F32)

    outgoing = dot(pick.astype(BF16), hidden.astype(BF16), 0, 0).astype(BF16)
    disp[...] = outgoing.reshape(NCTX, QS * CAP, LANES)
    arrived[me_c] = disp[me_c]

    def to_all(src, dst, sems):
        def copy(d):
            to = (me_c + d) % NCTX
            return pltpu.make_async_remote_copy(
                src_ref=src.at[to], dst_ref=dst.at[me_c], send_sem=sems.at[0, d],
                recv_sem=sems.at[1, d], device_id={"ctx": to}, device_id_type=MESH,
            )

        def start(d, carry):
            copy(d).start()
            return carry

        def finish(d, carry):
            arrive(dst.at[(me_c + NCTX - d) % NCTX], sems, d)
            return carry

        def leave(d, carry):
            copy(d).wait_send()
            return carry

        return [lambda f=f: lax.fori_loop(1, NCTX, f, 0) for f in (start, finish, leave)]

    start, finish, leave_disp = to_all(disp, arrived, d_sem)
    start()
    loads[1].wait()
    loads[2].wait()
    finish()
    rows = dot(perm[...], arrived[...].reshape(PAD, LANES), 1, 0).astype(BF16)
    rows = jnp.concatenate([rows[q * SLOTS : (q + 1) * SLOTS] for q in range(QS)], axis=1)

    wide = 2 * LANES
    for d in FAR_FIRST:
        first = pl.multiple_of(((x + d) % NX) * wide, wide)
        gate = dot(rows, wgu[:, pl.ds(first, wide)], 1, 0).astype(BF16)
        up = dot(rows, wgu[:, pl.ds(FF + first, wide)], 1, 0).astype(BF16)
        for c in range(2):
            gu[d, c, 0:SLOTS, :] = gate[:, c * LANES : (c + 1) * LANES]
            gu[d, c, SLOTS : 2 * SLOTS, :] = up[:, c * LANES : (c + 1) * LANES]
        for c in range(2) if d else (1 - core,):
            send(gu.at[d, c], gu_recv.at[d * 2 + core], g_sem, d * 2 + c, d * 2 + core, near(d, c))
    sums = gu[0, core].astype(F32)
    for d in (0, 1, 3, 2):
        for c in range(2) if d else (1 - core,):
            arrive(gu_recv.at[d * 2 + c], g_sem, d * 2 + c)
            sums = sums + gu_recv[d * 2 + c].astype(F32)
    gz_send[...] = sums.astype(BF16)
    send(gz_send, gz_recv, gz_sem, 0, 0, partner)
    arrive(gz_recv, gz_sem, 0)
    sums = sums + gz_recv[...].astype(F32)
    gate, up = sums[0:SLOTS], sums[SLOTS : 2 * SLOTS]
    act[me_q] = (gate / (1.0 + jnp.exp(-gate)) * up).astype(BF16)
    for d in FAR_FIRST:
        for c in range(2) if d else (1 - core,):
            send(act.at[me_q], act.at[me_q], act_sem, d * 2 + c, d * 2 + core, near(d, c))
    loads[3].wait()
    for d in (0, 1, 3, 2):
        for c in range(2) if d else (1 - core,):
            arrive(act.at[((x + NX - d) % NX) * 2 + c], act_sem, d * 2 + c)
    hidden_units = jnp.concatenate([act[q] for q in range(2 * NX)], axis=1)
    down[:, 0:COLS] = dot(hidden_units, wd[...], 1, 0)

    result = jnp.concatenate([down[:, q * LANES : (q + 1) * LANES] for q in range(QS)], axis=0)
    packed = dot(perm_t[...], result.astype(BF16), 1, 0).astype(BF16)
    ret[...] = packed.reshape(NCTX, QS * CAP, LANES)
    ret_recv[me_c] = ret[me_c]
    start, finish, leave_ret = to_all(ret, ret_recv, r_sem)
    start()
    finish()
    returned = ret_recv[...].reshape(PAD, LANES)
    high, low = split(pick_weight)
    final = (hidden + dot(high, returned, 1, 0) + dot(low, returned, 1, 0)).astype(BF16)
    for q in range(QS):
        width = min(LANES, COLS - q * LANES)
        out[:, q * LANES : q * LANES + width] = final[q * ROW_DEV : (q + 1) * ROW_DEV, 0:width]

    for src, sems, n in sent:
        pltpu.make_async_remote_copy(
            src_ref=src, dst_ref=src, send_sem=sems.at[0, n], recv_sem=sems.at[1, n],
            device_id=partner, device_id_type=MESH,
        ).wait_send()
    leave_disp()
    leave_ret()


def per_device(
    q_nope, q_rope, w_uk, w_uv, prompt, w_out, residual, routes, route_scores,
    expert_gate, expert_up, expert_down,
):
    vmem, hbm = pl.BlockSpec(memory_space=pltpu.VMEM), pl.BlockSpec(memory_space=pl.ANY)
    dma = pltpu.SemaphoreType.DMA
    near = 2 * NX
    half = VDIM // 2
    scratch = [
        ((HEADS * VDIM, COLS), BF16),
        ((PAD, 2 * FF), BF16),
        ((FF, COLS), BF16),
        ((PAD, PAD), BF16),
        ((PAD, PAD), BF16),
        ((HEADS, 2, half, ROWS), BF16),
        ((HEADS, 8, ROWS), F32),
        ((near, half, ROWS), BF16),
        ((near, 8, ROWS), F32),
        ((half, ROWS), BF16),
        ((half, ROWS), BF16),
        ((8, ROWS), F32),
        ((8, ROWS), F32),
        ((near, half, ROWS), BF16),
        ((ROWS, PAD), F32),
        ((NY, ROWS, LANES), BF16),
        ((NY, ROWS, LANES), BF16),
        ((NZ, QS * ROW_DEV, LANES), BF16),
        ((NZ, QS * ROW_DEV, LANES), BF16),
        ((ROW_DEV, PAD), F32),
        ((NCTX, QS * CAP, LANES), BF16),
        ((NCTX, QS * CAP, LANES), BF16),
        ((NX, 2, 2 * SLOTS, LANES), BF16),
        ((near, 2 * SLOTS, LANES), BF16),
        ((2 * SLOTS, LANES), BF16),
        ((2 * SLOTS, LANES), BF16),
        ((near, SLOTS, LANES), BF16),
        ((SLOTS, PAD), F32),
        ((NCTX, QS * CAP, LANES), BF16),
        ((NCTX, QS * CAP, LANES), BF16),
    ]
    sems = [(4,)] + [(2, n) for n in (near, near, 2, near, NY, NZ, NCTX, near, 1, near, NCTX)]
    return pl.pallas_call(
        kernel,
        out_shape=jax.ShapeDtypeStruct((ROW_DEV, COLS), BF16),
        in_specs=[vmem] * 8 + [hbm] * 4,
        out_specs=vmem,
        scratch_shapes=[pltpu.VMEM(*s) for s in scratch] + [dma(s) for s in sems],
        compiler_params=pltpu.CompilerParams(
            collective_id=0, has_side_effects=True, vmem_limit_bytes=48 * 2**20
        ),
        name="layer",
    )(
        jnp.transpose(q_nope, (1, 0, 2)),
        jnp.transpose(q_rope, (1, 0, 2)),
        w_uk, w_uv, prompt, residual, routes, route_scores, w_out,
        expert_gate[0], expert_up[0], expert_down[0],
    )


def solution(mesh):
    in_specs = (
        P(None, "ctx", None),
        P(None, "ctx", None),
        P("ctx", None, None),
        P("ctx", None, None),
        P("grp", None),
        P("ctx", "grp"),
        P("ctx", "grp"),
        P("ctx", None),
        P("ctx", None),
        P("ctx", "grp", None),
        P("ctx", "grp", None),
        P("ctx", None, "grp"),
    )
    return jax.shard_map(
        per_device, mesh=mesh, in_specs=in_specs, out_specs=P("ctx", "grp"), check_vma=False
    )
```

time: 794 us -> 97.8 us (0.12)
  waiting for transfers between devices: 704 us -> 0 us
  Pallas kernels: 0 us -> 88.5 us
  blocking collectives: 50.5 us -> 0 us
  matrix products: 15.5 us -> 0 us
  between operations: 13.2 us -> 0.12 us
    psum x1 -> x0, waiting for transfers between devices: 307 us -> none  [per_device(): gate_sum, up_sum = lax.psum((gate_part, up_part), 'grp')]
    reduce_scatter x1 -> x0, waiting for transfers between devices: 211 us -> none  [per_device(): lax.psum_scatter(jnp.dot(attended, w_out, preferred_element_type=jnp.floa...]
    all_gather x1 -> x0, waiting for transfers between devices: 173 us -> none  [per_device(): all_keys = lax.all_gather(prompt, 'grp', axis=0, tiled=True)]
    pallas_call x0 -> x1, Pallas kernels: none -> 88.5 us  [per_device(): pl.pallas_call(kernel, out_shape=jax.ShapeDtypeStruct((ROW_DEV, COLS), BF...]
    all_gather x1 -> x0, blocking collectives: 35.4 us -> none  [per_device(): attended = lax.all_gather(own_rows, 'grp', axis=0, tiled=True)]
    dot_general x12 -> x0, matrix products: 15.5 us -> none  [the longest x1 4.36 us: per_device(): jnp.einsum('rhc,jc->rhj', own_queries, all_keys, preferred_element_type=j...]
    all_to_all x1 -> x0, blocking collectives: 15.1 us -> none  [per_device(): lax.all_to_all(outgoing, 'ctx', split_axis=0, concat_axis=1, tiled=True)]
    all_to_all x1 -> x0, waiting for transfers between devices: 11.7 us -> none  [per_device(): lax.all_to_all(result, 'ctx', split_axis=1, concat_axis=0, tiled=True)]
  transfers between devices with their start and end apart: 4 -> 0, of which waited for: 4 -> 0; matrix products, arithmetic and copies ran while one was open for 0% -> 0% of each run, Pallas kernels for 0% -> 0%
where the time goes in v1:
time: 97.8 us; the launch traced here: 97.4 us
  Pallas kernels  88.5 us (90%)
  local copies, waits for them, and re-layouts  8.75 us (9%)
    pallas_call x1, Pallas kernels, per_device(): pl.pallas_call(kernel, out_shape=jax.ShapeDtypeStruct((ROW_DEV, COLS), BF...  88.5 us
    unnamed x24, local copies, waits for them, and re-layouts  8.75 us

profile of v1, /device:TPU:1, one launch (start us, length us, event | category | flops | bytes accessed | tf_op | source)
XLA Modules:
  0.0 97.4 jit_solution(2802288698204108661)
XLA Ops:
  0.0 0.0 copy-start.8
  0.0 1.0 %copy.19 = bf16[256,4,128]{2,0,1:T(8,128)(2,1)S(1)} copy(bf16[256,4,128]{2,1,0:T(4,128)(2,1)} %param.12) | data formatting | bytes 524288 | tf_op args[0]
  1.0 1.1 %copy.14 = bf16[256,4,64]{2,0,1:T(8,128)(2,1)S(1)} copy(bf16[256,4,64]{0,2,1:T(8,128)(2,1)} %param.13) | data formatting | bytes 262144 | tf_op args[1]
  2.1 0.0 copy-done.8
  2.1 0.0 copy-start.7
  2.1 0.3 copy.16.prompt
  2.4 0.7 copy-done.7
  3.2 0.2 copy.17.w_out_hbm
  3.4 0.0 copy-start
  3.4 0.0 copy-start.4
  3.4 0.0 copy-start.5
  3.4 0.0 copy-start.6
  3.4 1.5 %copy.15 = bf16[1,1024,448]{2,1,0:T(8,128)(2,1)S(1)} copy(bf16[1,1024,448]{1,2,0:T(8,128)(2,1)} %param.23) | data formatting | bytes 1835008 | tf_op args[11]
  5.0 0.0 copy-done
  5.0 0.0 copy-done.4
  5.0 0.0 copy-done.5
  5.0 0.0 copy-done.6
  5.0 0.0 copy-start.1
  5.0 1.2 %copy-done.1 = bf16[1,448,1024]{2,1,0:T(8,128)(2,1)S(1)} copy-done((bf16[1,448,1024]{2,1,0:T(8,128)(2,1)S(1)}, bf16[1,448,1024]{2,1,0:T(8,128)(2,1)}, u32[]{:S(2)}) %copy-start.1) | copy-done | bytes 917528
  6.2 0.0 copy-start.2
  6.2 1.0 %copy-done.2 = bf16[4,128,512]{2,1,0:T(8,128)(2,1)S(1)} copy-done((bf16[4,128,512]{2,1,0:T(8,128)(2,1)S(1)}, bf16[4,128,512]{2,1,0:T(8,128)(2,1)}, u32[]{:S(2)}) %copy-start.2) | copy-done | bytes 524312
  7.2 0.0 copy-start.3
  7.2 1.0 %copy-done.3 = bf16[4,512,128]{2,1,0:T(8,128)(2,1)S(1)} copy-done((bf16[4,512,128]{2,1,0:T(8,128)(2,1)S(1)}, bf16[4,512,128]{2,1,0:T(8,128)(2,1)}, u32[]{:S(2)}) %copy-start.3) | copy-done | bytes 524312
  8.3 88.5 %layer.1 = bf16[8,448]{1,0:T(8,128)(2,1)S(1)} custom-call(bf16[4,256,128]{2,1,0:T(8,128)(2,1)S(1)} %bitcast.8, bf16[4,256,64]{2,1,0:T(8,128)(2,1)S(1)} %bitcast.9, bf16[4,128,512]{2,1,0:T(8,128)(2,1)S(1)} %copy-done.2, bf16[4,512,128]{2,1,0:T(8,128)(2,1)S(1)} %copy-done.3, bf16[384,576]{1,0:T(8,128)(2,1)S(1)} %copy.16.prompt, bf16[8,448]{1,0:T(8,128)(2,1)S(1)} %copy-done.4, ...), custom_call_target="tpu_custom_call" | custom-call | tf_op jit(solution)/shard_map/layer/pallas_call | solution.py:350
  96.8 0.6 copy.21
Async XLA Ops:
  0.0 2.1 %copy-start.8 = (bf16[384,576]{0,1:T(8,128)(2,1)S(1)}, bf16[384,576]{0,1:T(8,128)(2,1)}, u32[]{:S(2)}) copy-start(bf16[384,576]{0,1:T(8,128)(2,1)} %param.16) | copy-start | bytes 1327108
  2.1 1.0 %copy-start.7 = (bf16[512,448]{0,1:T(8,128)(2,1)S(1)}, bf16[512,448]{0,1:T(8,128)(2,1)}, u32[]{:S(2)}) copy-start(bf16[512,448]{0,1:T(8,128)(2,1)} %param.17) | copy-start | bytes 1376260
  3.4 1.6 %copy-start = (bf16[1,448,1024]{2,1,0:T(8,128)(2,1)S(1)}, bf16[1,448,1024]{2,1,0:T(8,128)(2,1)}, u32[]{:S(2)}) copy-start(bf16[1,448,1024]{2,1,0:T(8,128)(2,1)} %param.21) | copy-start | bytes 2752516
  3.4 1.6 %copy-start.4 = (bf16[8,448]{1,0:T(8,128)(2,1)S(1)}, bf16[8,448]{1,0:T(8,128)(2,1)}, u32[]{:S(2)}) copy-start(bf16[8,448]{1,0:T(8,128)(2,1)} %residual.1) | copy-start | bytes 21508
  3.4 1.6 %copy-start.5 = (s32[8,8]{1,0:T(8,128)S(1)}, s32[8,8]{1,0:T(8,128)}, u32[]{:S(2)}) copy-start(s32[8,8]{1,0:T(8,128)} %routes.1) | copy-start | bytes 772
  3.4 1.6 %copy-start.6 = (f32[8,8]{1,0:T(8,128)S(1)}, f32[8,8]{1,0:T(8,128)}, u32[]{:S(2)}) copy-start(f32[8,8]{1,0:T(8,128)} %scores.1) | copy-start | bytes 772
  5.0 1.2 %copy-start.1 = (bf16[1,448,1024]{2,1,0:T(8,128)(2,1)S(1)}, bf16[1,448,1024]{2,1,0:T(8,128)(2,1)}, u32[]{:S(2)}) copy-start(bf16[1,448,1024]{2,1,0:T(8,128)(2,1)} %param.22) | copy-start | bytes 2752516
  6.2 1.0 %copy-start.2 = (bf16[4,128,512]{2,1,0:T(8,128)(2,1)S(1)}, bf16[4,128,512]{2,1,0:T(8,128)(2,1)}, u32[]{:S(2)}) copy-start(bf16[4,128,512]{2,1,0:T(8,128)(2,1)} %w_uk.1) | copy-start | bytes 1572868
  7.2 1.0 %copy-start.3 = (bf16[4,512,128]{2,1,0:T(8,128)(2,1)S(1)}, bf16[4,512,128]{2,1,0:T(8,128)(2,1)}, u32[]{:S(2)}) copy-start(bf16[4,512,128]{2,1,0:T(8,128)(2,1)} %w_uv.1) | copy-start | bytes 1572868

commit v2 on v1

--- a/solution.py
+++ b/solution.py
@@ -40,8 +40,10 @@
 
 
 def kernel(
-    qn, qr, w_uk, w_uv, prompt, residual, routes, scores, w_out_hbm, wg_hbm, wu_hbm, wd_hbm,
+    residual, routes, scores,
+    qn_hbm, qr_hbm, w_uk_hbm, w_uv_hbm, prompt_hbm, w_out_hbm, wg_hbm, wu_hbm, wd_hbm,
     out,
+    qn, q_wide, qr, w_uk, w_uv, prompt, keys,
     w_out, wgu, wd, perm, perm_t,
     obuf, lse, o_recv, l_recv, zh_send, zh_recv, zl_send, zl_recv, att,
     proj, pbuf, p_recv, zbuf, z_recv, res_pad, disp, arrived,
@@ -58,6 +60,20 @@
     def near(d, c):
         return {"grp": ((x + d) % NX) * 4 + zh * 2 + c}
 
+    pairs = (
+        (prompt_hbm, prompt),
+        (qn_hbm, qn),
+        (w_uk_hbm, w_uk),
+        (qr_hbm, qr),
+        (w_uv_hbm, w_uv),
+        (w_out_hbm, w_out),
+        (wg_hbm, wgu.at[pl.ds(0, COLS), pl.ds(0, FF)]),
+        (wu_hbm, wgu.at[pl.ds(0, COLS), pl.ds(FF, FF)]),
+        (wd_hbm, wd),
+    )
+    loads = [pltpu.make_async_copy(a, b, load_sem.at[i]) for i, (a, b) in enumerate(pairs)]
+    for load in loads:
+        load.start()
     barrier = pltpu.get_barrier_semaphore()
     for d in range(NX):
         if d:
@@ -74,14 +90,6 @@
 
     lax.fori_loop(1, NCTX, greet, 0)
 
-    loads = [
-        pltpu.make_async_copy(w_out_hbm, w_out, load_sem.at[0]),
-        pltpu.make_async_copy(wg_hbm, wgu.at[pl.ds(0, COLS), pl.ds(0, FF)], load_sem.at[1]),
-        pltpu.make_async_copy(wu_hbm, wgu.at[pl.ds(0, COLS), pl.ds(FF, FF)], load_sem.at[2]),
-        pltpu.make_async_copy(wd_hbm, wd, load_sem.at[3]),
-    ]
-    for load in loads:
-        load.start()
     sent = []
 
     def send(src, dst, sems, n, at, device):
@@ -99,16 +107,19 @@
         ).wait_recv()
 
     scale = (NOPE + ROPE) ** -0.5
-    latents = prompt[:, 0:LAT]
-    rotated = prompt[:, LAT : LAT + ROPE]
+    for load in loads[0:5]:
+        load.wait()
+    keys[...] = prompt[...].T
+    q_wide[...] = qn[...].astype(F32)
     for step, d in enumerate(FAR_FIRST):
         h = (x + d) % NX
-        q_latent = dot(qn[h], w_uk[h], 1, 0).astype(BF16)
-        s = (dot(latents, q_latent, 1, 1) + dot(rotated, qr[h], 1, 1)) * scale
+        q = q_wide[pl.ds(h, ROWS, stride=HEADS), :].astype(BF16)
+        queries = jnp.concatenate([dot(w_uk[h], q, 0, 1).astype(BF16), qr[h]], axis=0)
+        s = dot(keys[...], queries, 1, 0) * scale
         top = jnp.max(s, axis=0, keepdims=True)
         raised = jnp.exp(s - top)
         total = jnp.sum(raised, axis=0, keepdims=True)
-        weighted = dot(latents, raised.astype(BF16), 0, 0)
+        weighted = dot(prompt[0:LAT, :], raised.astype(BF16), 1, 0)
         high, low = split(weighted)
         values = dot(w_uv[h], high, 0, 0) + dot(w_uv[h], low, 0, 0)
         o = (values / total).astype(BF16)
@@ -193,8 +204,8 @@
         for c in range(2) if d else (1 - core,):
             arrive(att.at[((x + NX - d) % NX) * 2 + c], ag_sem, d * 2 + c)
 
-    loads[0].wait()
-    proj[:, 0:COLS] = dot(att[...].reshape(HEADS * VDIM, ROWS), w_out[...], 0, 0)
+    loads[5].wait()
+    proj[:, 0:COLS] = dot(att[...].reshape(HEADS * VDIM, ROWS), w_out[...], 0, 1)
     for to in range(NY):
         parts = []
         for q in range(QS):
@@ -246,8 +257,8 @@
 
     start, finish, leave_disp = to_all(disp, arrived, d_sem)
     start()
-    loads[1].wait()
-    loads[2].wait()
+    loads[6].wait()
+    loads[7].wait()
     finish()
     rows = dot(perm[...], arrived[...].reshape(PAD, LANES), 1, 0).astype(BF16)
     rows = jnp.concatenate([rows[q * SLOTS : (q + 1) * SLOTS] for q in range(QS)], axis=1)
@@ -276,12 +287,12 @@
     for d in FAR_FIRST:
         for c in range(2) if d else (1 - core,):
             send(act.at[me_q], act.at[me_q], act_sem, d * 2 + c, d * 2 + core, near(d, c))
-    loads[3].wait()
+    loads[8].wait()
     for d in (0, 1, 3, 2):
         for c in range(2) if d else (1 - core,):
             arrive(act.at[((x + NX - d) % NX) * 2 + c], act_sem, d * 2 + c)
     hidden_units = jnp.concatenate([act[q] for q in range(2 * NX)], axis=1)
-    down[:, 0:COLS] = dot(hidden_units, wd[...], 1, 0)
+    down[:, 0:COLS] = dot(hidden_units, wd[...], 1, 1)
 
     result = jnp.concatenate([down[:, q * LANES : (q + 1) * LANES] for q in range(QS)], axis=0)
     packed = dot(perm_t[...], result.astype(BF16), 1, 0).astype(BF16)
@@ -315,9 +326,16 @@
     near = 2 * NX
     half = VDIM // 2
     scratch = [
-        ((HEADS * VDIM, COLS), BF16),
+        ((ROWS * HEADS, NOPE), BF16),
+        ((ROWS * HEADS, NOPE), F32),
+        ((HEADS, ROPE, ROWS), BF16),
+        ((HEADS, NOPE, LAT), BF16),
+        ((HEADS, LAT, VDIM), BF16),
+        ((LAT + ROPE, KEYS), BF16),
+        ((KEYS, LAT + ROPE), BF16),
+        ((COLS, HEADS * VDIM), BF16),
         ((PAD, 2 * FF), BF16),
-        ((FF, COLS), BF16),
+        ((COLS, FF), BF16),
         ((PAD, PAD), BF16),
         ((PAD, PAD), BF16),
         ((HEADS, 2, half, ROWS), BF16),
@@ -346,22 +364,21 @@
         ((NCTX, QS * CAP, LANES), BF16),
         ((NCTX, QS * CAP, LANES), BF16),
     ]
-    sems = [(4,)] + [(2, n) for n in (near, near, 2, near, NY, NZ, NCTX, near, 1, near, NCTX)]
+    sems = [(9,)] + [(2, n) for n in (near, near, 2, near, NY, NZ, NCTX, near, 1, near, NCTX)]
     return pl.pallas_call(
         kernel,
         out_shape=jax.ShapeDtypeStruct((ROW_DEV, COLS), BF16),
-        in_specs=[vmem] * 8 + [hbm] * 4,
+        in_specs=[vmem] * 3 + [hbm] * 9,
         out_specs=vmem,
         scratch_shapes=[pltpu.VMEM(*s) for s in scratch] + [dma(s) for s in sems],
         compiler_params=pltpu.CompilerParams(
-            collective_id=0, has_side_effects=True, vmem_limit_bytes=48 * 2**20
+            collective_id=0, has_side_effects=True, vmem_limit_bytes=60 * 2**20
         ),
         name="layer",
     )(
-        jnp.transpose(q_nope, (1, 0, 2)),
-        jnp.transpose(q_rope, (1, 0, 2)),
-        w_uk, w_uv, prompt, residual, routes, route_scores, w_out,
-        expert_gate[0], expert_up[0], expert_down[0],
+        residual, routes, route_scores,
+        q_nope.reshape(ROWS * HEADS, NOPE), jnp.transpose(q_rope, (1, 2, 0)), w_uk, w_uv, prompt.T,
+        w_out.T, expert_gate[0], expert_up[0], expert_down[0].T,
     )
 
 

time: 97.8 us -> 91.7 us (0.938)
  local copies, waits for them, and re-layouts: 8.75 us -> 1.3 us
  Pallas kernels: 88.5 us -> 90.2 us
    unnamed x24 -> x1, local copies, waits for them, and re-layouts: 8.75 us -> 1.3 us
    pallas_call x1, Pallas kernels: 88.5 us -> 90.2 us  [per_device(): pl.pallas_call(kernel, out_shape=jax.ShapeDtypeStruct((ROW_DEV, COLS), BF...]
where the time goes in v2:
time: 91.7 us; the launch traced here: 91.5 us
  Pallas kernels  90.2 us (98%)
  local copies, waits for them, and re-layouts  1.3 us (1%)
    pallas_call x1, Pallas kernels, per_device(): pl.pallas_call(kernel, out_shape=jax.ShapeDtypeStruct((ROW_DEV, COLS), BF...  90.2 us

profile of v2, /device:TPU:1, one launch (start us, length us, event | category | flops | bytes accessed | tf_op | source)
XLA Modules:
  0.0 91.5 jit_solution(5558404192627814993)
XLA Ops:
  0.0 90.2 %layer.1 = bf16[8,448]{1,0:T(8,128)(2,1)} custom-call(bf16[8,448]{1,0:T(8,128)(2,1)} %residual.1, s32[8,8]{1,0:T(8,128)} %routes.1, f32[8,8]{1,0:T(8,128)} %scores.1, bf16[1024,128]{1,0:T(8,128)(2,1)} %bitcast.14, bf16[4,64,256]{2,1,0:T(8,128)(2,1)} %bitcast.15, bf16[4,128,512]{2,1,0:T(8,128)(2,1)} %w_uk_hbm.1, bf16[4,512,128]{2,1,0:T(8,128)(2,1)} %w_uv_hbm.1, ...), custom_call_target="tpu_custom_call" | custom-call | tf_op jit(solution)/shard_map/layer/pallas_call | solution.py:368
  90.2 1.3 %copy.14 = bf16[8,448]{1,0:T(8,128)(2,1)} copy(bf16[8,448]{1,0:T(8,128)(2,1)} %layer.1) | data formatting | bytes 14336

commit v3 on v2

--- a/solution.py
+++ b/solution.py
@@ -25,6 +25,7 @@
 SLOTS = NCTX * CAP
 ROUTE_FACTOR = 2.5
 FAR_FIRST = (2, 1, 3, 0)
+OFFSETS = [(dz, dy) for dz in (4, 3, 5, 2, 6, 1, 7, 0) for dy in FAR_FIRST][:-1]
 F32 = jnp.float32
 BF16 = jnp.bfloat16
 MESH = pl.DeviceIdType.MESH
@@ -47,8 +48,8 @@
     w_out, wgu, wd, perm, perm_t,
     obuf, lse, o_recv, l_recv, zh_send, zh_recv, zl_send, zl_recv, att,
     proj, pbuf, p_recv, zbuf, z_recv, res_pad, disp, arrived,
-    gu, gu_recv, gz_send, gz_recv, act, down, ret, ret_recv,
-    load_sem, o_sem, l_sem, zh_sem, ag_sem, y_sem, z_sem, d_sem, g_sem, gz_sem, act_sem, r_sem,
+    gu_own, gu_send, gu_recv, gx_send, gx_recv, gz_send, gz_recv, act, down, ret, ret_recv,
+    load_sem, o_sem, l_sem, zh_sem, ag_sem, y_sem, z_sem, d_sem, gs_sem, g_sem, gz_sem, act_sem, r_sem,
 ):
     me_c = lax.axis_index("ctx")
     me_g = lax.axis_index("grp")
@@ -75,21 +76,13 @@
     for load in loads:
         load.start()
     barrier = pltpu.get_barrier_semaphore()
-    for d in range(NX):
-        if d:
-            for c in range(2):
-                pl.semaphore_signal(barrier, inc=1, device_id=near(d, c), device_id_type=MESH)
-    pl.semaphore_signal(barrier, inc=1, device_id=near(0, 1 - core), device_id_type=MESH)
-    pl.semaphore_signal(barrier, inc=1, device_id=partner, device_id_type=MESH)
-
-    def greet(d, carry):
-        pl.semaphore_signal(
-            barrier, inc=1, device_id={"ctx": (me_c + d) % NCTX}, device_id_type=MESH
-        )
-        return carry
-
-    lax.fori_loop(1, NCTX, greet, 0)
-
+    sibling = near(0, 1 - core)
+    others = [((z + dz) % NZ) * NY + (y + dy) % NY for dz, dy in OFFSETS]
+    sources = [((z + NZ - dz) % NZ) * NY + (y + NY - dy) % NY for dz, dy in OFFSETS]
+    greeted = [partner] + [{"ctx": c} for c in others]
+    greeted += [near(d, c) for d in FAR_FIRST[:3] for c in range(2)] + [sibling]
+    for device in greeted:
+        pl.semaphore_signal(barrier, inc=1, device_id=device, device_id_type=MESH)
     sent = []
 
     def send(src, dst, sems, n, at, device):
@@ -106,13 +99,23 @@
             device_id=partner, device_id_type=MESH,
         ).wait_recv()
 
+    def spread(buf, sems):
+        for d in (2, 1, 3):
+            send(buf.at[me_q], buf.at[me_q], sems, d, d, near(d, core))
+        send(buf.at[me_q], buf.at[me_q], sems, NX, NX, sibling)
+        for d in (1, 3, 2):
+            got = ((x + NX - d) % NX) * 2 + core
+            arrive(buf.at[got], sems, d)
+            send(buf.at[got], buf.at[got], sems, NX + d, NX + d, sibling)
+        for d in (0, 1, 3, 2):
+            arrive(buf.at[((x + NX - d) % NX) * 2 + 1 - core], sems, NX + d)
+
     scale = (NOPE + ROPE) ** -0.5
     for load in loads[0:5]:
         load.wait()
     keys[...] = prompt[...].T
     q_wide[...] = qn[...].astype(F32)
-    for step, d in enumerate(FAR_FIRST):
-        h = (x + d) % NX
+    for h in range(HEADS):
         q = q_wide[pl.ds(h, ROWS, stride=HEADS), :].astype(BF16)
         queries = jnp.concatenate([dot(w_uk[h], q, 0, 1).astype(BF16), qr[h]], axis=0)
         s = dot(keys[...], queries, 1, 0) * scale
@@ -125,14 +128,14 @@
         o = (values / total).astype(BF16)
         obuf[h] = o.reshape(2, VDIM // 2, ROWS)
         lse[h] = jnp.broadcast_to(top + jnp.log(total), (8, ROWS))
-        if step == 0:
-            pl.semaphore_wait(barrier, 2 * NX - 1 + 1 + NCTX - 1)
+    pl.semaphore_wait(barrier, len(greeted))
+    for d in FAR_FIRST:
+        h = (x + d) % NX
         for c in range(2) if d else (1 - core,):
             send(obuf.at[h, c], o_recv.at[d * 2 + core], o_sem, d * 2 + c, d * 2 + core, near(d, c))
             send(lse.at[h], l_recv.at[d * 2 + core], l_sem, d * 2 + c, d * 2 + core, near(d, c))
-        if d == 0:
-            o_recv[core] = obuf[h, core]
-            l_recv[core] = lse[h]
+    o_recv[core] = obuf[x, core]
+    l_recv[core] = lse[x]
 
     wgu[COLS:PAD, :] = jnp.zeros((PAD - COLS, 2 * FF), BF16)
     slot = lax.broadcasted_iota(jnp.int32, (PAD, PAD), 0)
@@ -197,12 +200,7 @@
     arrive(zl_recv, zh_sem, 1)
     o, _ = merge([zh_send[...], zh_recv[...]], [l, zl_recv[0:1, :]])
     att[me_q] = o.astype(BF16)
-    for d in FAR_FIRST:
-        for c in range(2) if d else (1 - core,):
-            send(att.at[me_q], att.at[me_q], ag_sem, d * 2 + c, d * 2 + core, near(d, c))
-    for d in FAR_FIRST:
-        for c in range(2) if d else (1 - core,):
-            arrive(att.at[((x + NX - d) % NX) * 2 + c], ag_sem, d * 2 + c)
+    spread(att, ag_sem)
 
     loads[5].wait()
     proj[:, 0:COLS] = dot(att[...].reshape(HEADS * VDIM, ROWS), w_out[...], 0, 1)
@@ -231,76 +229,57 @@
 
     outgoing = dot(pick.astype(BF16), hidden.astype(BF16), 0, 0).astype(BF16)
     disp[...] = outgoing.reshape(NCTX, QS * CAP, LANES)
-    arrived[me_c] = disp[me_c]
-
     def to_all(src, dst, sems):
-        def copy(d):
-            to = (me_c + d) % NCTX
-            return pltpu.make_async_remote_copy(
-                src_ref=src.at[to], dst_ref=dst.at[me_c], send_sem=sems.at[0, d],
-                recv_sem=sems.at[1, d], device_id={"ctx": to}, device_id_type=MESH,
-            )
-
-        def start(d, carry):
-            copy(d).start()
-            return carry
-
-        def finish(d, carry):
-            arrive(dst.at[(me_c + NCTX - d) % NCTX], sems, d)
-            return carry
-
-        def leave(d, carry):
-            copy(d).wait_send()
-            return carry
-
-        return [lambda f=f: lax.fori_loop(1, NCTX, f, 0) for f in (start, finish, leave)]
-
-    start, finish, leave_disp = to_all(disp, arrived, d_sem)
-    start()
+        dst[me_c] = src[me_c]
+        for n, to in enumerate(others):
+            send(src.at[to], dst.at[me_c], sems, n, n, {"ctx": to})
+
+    def from_all(dst, sems):
+        for n, source in enumerate(sources):
+            arrive(dst.at[source], sems, n)
+
+    to_all(disp, arrived, d_sem)
     loads[6].wait()
     loads[7].wait()
-    finish()
+    from_all(arrived, d_sem)
     rows = dot(perm[...], arrived[...].reshape(PAD, LANES), 1, 0).astype(BF16)
     rows = jnp.concatenate([rows[q * SLOTS : (q + 1) * SLOTS] for q in range(QS)], axis=1)
 
     wide = 2 * LANES
     for d in FAR_FIRST:
         first = pl.multiple_of(((x + d) % NX) * wide, wide)
-        gate = dot(rows, wgu[:, pl.ds(first, wide)], 1, 0).astype(BF16)
-        up = dot(rows, wgu[:, pl.ds(FF + first, wide)], 1, 0).astype(BF16)
-        for c in range(2):
-            gu[d, c, 0:SLOTS, :] = gate[:, c * LANES : (c + 1) * LANES]
-            gu[d, c, SLOTS : 2 * SLOTS, :] = up[:, c * LANES : (c + 1) * LANES]
-        for c in range(2) if d else (1 - core,):
-            send(gu.at[d, c], gu_recv.at[d * 2 + core], g_sem, d * 2 + c, d * 2 + core, near(d, c))
-    sums = gu[0, core].astype(F32)
-    for d in (0, 1, 3, 2):
-        for c in range(2) if d else (1 - core,):
-            arrive(gu_recv.at[d * 2 + c], g_sem, d * 2 + c)
-            sums = sums + gu_recv[d * 2 + c].astype(F32)
+        gate = dot(rows, wgu[:, pl.ds(first, wide)], 1, 0)
+        up = dot(rows, wgu[:, pl.ds(FF + first, wide)], 1, 0)
+        even = jnp.concatenate([gate[:, 0:LANES], up[:, 0:LANES]], axis=0)
+        odd = jnp.concatenate([gate[:, LANES:wide], up[:, LANES:wide]], axis=0)
+        gu_own[d] = jnp.where(core == 0, even, odd)
+        gu_send[d] = jnp.where(core == 0, odd, even).astype(BF16)
+        send(gu_send.at[d], gu_recv.at[d], gs_sem, d, d, sibling)
+    for d in (2, 1, 3):
+        arrive(gu_recv.at[d], gs_sem, d)
+        gx_send[d] = (gu_own[d] + gu_recv[d].astype(F32)).astype(BF16)
+        send(gx_send.at[d], gx_recv.at[d], g_sem, d, d, near(d, core))
+    arrive(gu_recv.at[0], gs_sem, 0)
+    sums = gu_own[0] + gu_recv[0].astype(F32)
+    for d in (1, 3, 2):
+        arrive(gx_recv.at[d], g_sem, d)
+        sums = sums + gx_recv[d].astype(F32)
     gz_send[...] = sums.astype(BF16)
     send(gz_send, gz_recv, gz_sem, 0, 0, partner)
     arrive(gz_recv, gz_sem, 0)
     sums = sums + gz_recv[...].astype(F32)
     gate, up = sums[0:SLOTS], sums[SLOTS : 2 * SLOTS]
     act[me_q] = (gate / (1.0 + jnp.exp(-gate)) * up).astype(BF16)
-    for d in FAR_FIRST:
-        for c in range(2) if d else (1 - core,):
-            send(act.at[me_q], act.at[me_q], act_sem, d * 2 + c, d * 2 + core, near(d, c))
     loads[8].wait()
-    for d in (0, 1, 3, 2):
-        for c in range(2) if d else (1 - core,):
-            arrive(act.at[((x + NX - d) % NX) * 2 + c], act_sem, d * 2 + c)
+    spread(act, act_sem)
     hidden_units = jnp.concatenate([act[q] for q in range(2 * NX)], axis=1)
     down[:, 0:COLS] = dot(hidden_units, wd[...], 1, 1)
 
     result = jnp.concatenate([down[:, q * LANES : (q + 1) * LANES] for q in range(QS)], axis=0)
     packed = dot(perm_t[...], result.astype(BF16), 1, 0).astype(BF16)
     ret[...] = packed.reshape(NCTX, QS * CAP, LANES)
-    ret_recv[me_c] = ret[me_c]
-    start, finish, leave_ret = to_all(ret, ret_recv, r_sem)
-    start()
-    finish()
+    to_all(ret, ret_recv, r_sem)
+    from_all(ret_recv, r_sem)
     returned = ret_recv[...].reshape(PAD, LANES)
     high, low = split(pick_weight)
     final = (hidden + dot(high, returned, 1, 0) + dot(low, returned, 1, 0)).astype(BF16)
@@ -313,8 +292,6 @@
             src_ref=src, dst_ref=src, send_sem=sems.at[0, n], recv_sem=sems.at[1, n],
             device_id=partner, device_id_type=MESH,
         ).wait_send()
-    leave_disp()
-    leave_ret()
 
 
 def per_device(
@@ -355,8 +332,11 @@
         ((ROW_DEV, PAD), F32),
         ((NCTX, QS * CAP, LANES), BF16),
         ((NCTX, QS * CAP, LANES), BF16),
-        ((NX, 2, 2 * SLOTS, LANES), BF16),
-        ((near, 2 * SLOTS, LANES), BF16),
+        ((NX, 2 * SLOTS, LANES), F32),
+        ((NX, 2 * SLOTS, LANES), BF16),
+        ((NX, 2 * SLOTS, LANES), BF16),
+        ((NX, 2 * SLOTS, LANES), BF16),
+        ((NX, 2 * SLOTS, LANES), BF16),
         ((2 * SLOTS, LANES), BF16),
         ((2 * SLOTS, LANES), BF16),
         ((near, SLOTS, LANES), BF16),
@@ -364,10 +344,10 @@
         ((NCTX, QS * CAP, LANES), BF16),
         ((NCTX, QS * CAP, LANES), BF16),
     ]
-    sems = [(9,)] + [(2, n) for n in (near, near, 2, near, NY, NZ, NCTX, near, 1, near, NCTX)]
+    sems = [(9,)] + [(2, n) for n in (near, near, 2, near, NY, NZ, NCTX, NX, NX, 1, near, NCTX)]
     return pl.pallas_call(
         kernel,
-        out_shape=jax.ShapeDtypeStruct((ROW_DEV, COLS), BF16),
+        out_shape=pltpu.VMEM((ROW_DEV, COLS), BF16),
         in_specs=[vmem] * 3 + [hbm] * 9,
         out_specs=vmem,
         scratch_shapes=[pltpu.VMEM(*s) for s in scratch] + [dma(s) for s in sems],

time: 91.7 us -> 89 us (0.971)
  Pallas kernels: 90.2 us -> 88.3 us
    pallas_call x1, Pallas kernels: 90.2 us -> 88.3 us  [per_device(): pl.pallas_call(kernel, out_shape=pltpu.VMEM((ROW_DEV, COLS), BF16), in_sp...]
where the time goes in v3:
time: 89 us; the launch traced here: 88.9 us
  Pallas kernels  88.3 us (99%)
    pallas_call x1, Pallas kernels, per_device(): pl.pallas_call(kernel, out_shape=pltpu.VMEM((ROW_DEV, COLS), BF16), in_sp...  88.3 us

profile of v3, /device:TPU:1, one launch (start us, length us, event | category | flops | bytes accessed | tf_op | source)
XLA Modules:
  0.0 88.9 jit_solution(10277342767088448289)
XLA Ops:
  0.0 88.3 %layer.1 = bf16[8,448]{1,0:T(8,128)(2,1)S(1)} custom-call(bf16[8,448]{1,0:T(8,128)(2,1)} %residual.1, s32[8,8]{1,0:T(8,128)} %routes.1, f32[8,8]{1,0:T(8,128)} %scores.1, bf16[1024,128]{1,0:T(8,128)(2,1)} %bitcast.14, bf16[4,64,256]{2,1,0:T(8,128)(2,1)} %bitcast.15, bf16[4,128,512]{2,1,0:T(8,128)(2,1)} %w_uk_hbm.1, bf16[4,512,128]{2,1,0:T(8,128)(2,1)} %w_uv_hbm.1, ...), custom_call_target="tpu_custom_call" | custom-call | tf_op jit(solution)/shard_map/layer/pallas_call | solution.py:348
  88.3 0.6 copy.14

commit v4 on v3

--- a/solution.py
+++ b/solution.py
@@ -45,7 +45,7 @@
     qn_hbm, qr_hbm, w_uk_hbm, w_uv_hbm, prompt_hbm, w_out_hbm, wg_hbm, wu_hbm, wd_hbm,
     out,
     qn, q_wide, qr, w_uk, w_uv, prompt, keys,
-    w_out, wgu, wd, perm, perm_t,
+    w_out, w_out_t, wgu, wd, wd_t, perm, perm_t,
     obuf, lse, o_recv, l_recv, zh_send, zh_recv, zl_send, zl_recv, att,
     proj, pbuf, p_recv, zbuf, z_recv, res_pad, disp, arrived,
     gu_own, gu_send, gu_recv, gx_send, gx_recv, gz_send, gz_recv, act, down, ret, ret_recv,
@@ -73,7 +73,7 @@
         (wd_hbm, wd),
     )
     loads = [pltpu.make_async_copy(a, b, load_sem.at[i]) for i, (a, b) in enumerate(pairs)]
-    for load in loads:
+    for load in loads[0:5]:
         load.start()
     barrier = pltpu.get_barrier_semaphore()
     sibling = near(0, 1 - core)
@@ -111,10 +111,14 @@
             arrive(buf.at[((x + NX - d) % NX) * 2 + 1 - core], sems, NX + d)
 
     scale = (NOPE + ROPE) ** -0.5
-    for load in loads[0:5]:
+    loads[0].wait()
+    keys[...] = prompt[...].T
+    loads[1].wait()
+    q_wide[...] = qn[...].astype(F32)
+    for load in loads[2:5]:
         load.wait()
-    keys[...] = prompt[...].T
-    q_wide[...] = qn[...].astype(F32)
+    for load in loads[5:9]:
+        load.start()
     for h in range(HEADS):
         q = q_wide[pl.ds(h, ROWS, stride=HEADS), :].astype(BF16)
         queries = jnp.concatenate([dot(w_uk[h], q, 0, 1).astype(BF16), qr[h]], axis=0)
@@ -173,6 +177,9 @@
         [jnp.where(block_of == q, picked * weight, 0.0) for q in range(QS)], axis=0
     )
 
+    loads[5].wait()
+    w_out_t[...] = w_out[...].T
+
     for d in FAR_FIRST:
         for c in range(2) if d else (1 - core,):
             arrive(o_recv.at[d * 2 + c], o_sem, d * 2 + c)
@@ -196,14 +203,15 @@
     zl_send[...] = jnp.broadcast_to(l, (8, ROWS))
     send(zh_send, zh_recv, zh_sem, 0, 0, partner)
     send(zl_send, zl_recv, zh_sem, 1, 1, partner)
+    loads[8].wait()
+    wd_t[...] = wd[...].T
     arrive(zh_recv, zh_sem, 0)
     arrive(zl_recv, zh_sem, 1)
     o, _ = merge([zh_send[...], zh_recv[...]], [l, zl_recv[0:1, :]])
     att[me_q] = o.astype(BF16)
     spread(att, ag_sem)
 
-    loads[5].wait()
-    proj[:, 0:COLS] = dot(att[...].reshape(HEADS * VDIM, ROWS), w_out[...], 0, 1)
+    proj[:, 0:COLS] = dot(att[...].reshape(HEADS * VDIM, ROWS), w_out_t[...], 0, 0)
     for to in range(NY):
         parts = []
         for q in range(QS):
@@ -270,10 +278,9 @@
     sums = sums + gz_recv[...].astype(F32)
     gate, up = sums[0:SLOTS], sums[SLOTS : 2 * SLOTS]
     act[me_q] = (gate / (1.0 + jnp.exp(-gate)) * up).astype(BF16)
-    loads[8].wait()
     spread(act, act_sem)
     hidden_units = jnp.concatenate([act[q] for q in range(2 * NX)], axis=1)
-    down[:, 0:COLS] = dot(hidden_units, wd[...], 1, 1)
+    down[:, 0:COLS] = dot(hidden_units, wd_t[...], 1, 0)
 
     result = jnp.concatenate([down[:, q * LANES : (q + 1) * LANES] for q in range(QS)], axis=0)
     packed = dot(perm_t[...], result.astype(BF16), 1, 0).astype(BF16)
@@ -311,8 +318,10 @@
         ((LAT + ROPE, KEYS), BF16),
         ((KEYS, LAT + ROPE), BF16),
         ((COLS, HEADS * VDIM), BF16),
+        ((HEADS * VDIM, COLS), BF16),
         ((PAD, 2 * FF), BF16),
         ((COLS, FF), BF16),
+        ((FF, COLS), BF16),
         ((PAD, PAD), BF16),
         ((PAD, PAD), BF16),
         ((HEADS, 2, half, ROWS), BF16),

time: 89 us -> 88.9 us (level)
  no operation moved by 1% of the time
where the time goes in v4:
time: 88.9 us; the launch traced here: 88.7 us
  Pallas kernels  88.1 us (99%)
    pallas_call x1, Pallas kernels, per_device(): pl.pallas_call(kernel, out_shape=pltpu.VMEM((ROW_DEV, COLS), BF16), in_sp...  88.1 us

profile of v4, /device:TPU:1, one launch (start us, length us, event | category | flops | bytes accessed | tf_op | source)
XLA Modules:
  0.0 88.7 jit_solution(15209859562957849846)
XLA Ops:
  0.0 88.1 %layer.1 = bf16[8,448]{1,0:T(8,128)(2,1)S(1)} custom-call(bf16[8,448]{1,0:T(8,128)(2,1)} %residual.1, s32[8,8]{1,0:T(8,128)} %routes.1, f32[8,8]{1,0:T(8,128)} %scores.1, bf16[1024,128]{1,0:T(8,128)(2,1)} %bitcast.14, bf16[4,64,256]{2,1,0:T(8,128)(2,1)} %bitcast.15, bf16[4,128,512]{2,1,0:T(8,128)(2,1)} %w_uk_hbm.1, bf16[4,512,128]{2,1,0:T(8,128)(2,1)} %w_uv_hbm.1, ...), custom_call_target="tpu_custom_call" | custom-call | tf_op jit(solution)/shard_map/layer/pallas_call | solution.py:357
  88.1 0.6 copy.14

commit v5 on v4

--- a/solution.py
+++ b/solution.py
@@ -20,6 +20,7 @@
 PAD = 512
 QS = PAD // LANES
 ROW_DEV = 8
+ROWS_Y = 64
 NZ, NY, NX = 8, 4, 4
 NCTX = NZ * NY
 SLOTS = NCTX * CAP
@@ -46,10 +47,10 @@
     out,
     qn, q_wide, qr, w_uk, w_uv, prompt, keys,
     w_out, w_out_t, wgu, wd, wd_t, perm, perm_t,
-    obuf, lse, o_recv, l_recv, zh_send, zh_recv, zl_send, zl_recv, att,
-    proj, pbuf, p_recv, zbuf, z_recv, res_pad, disp, arrived,
+    obuf, lse, o_recv, l_recv, zh_send, zh_recv, zl_send, zl_recv, att_send, att,
+    proj, zbuf, z_recv, res_pad, disp, arrived,
     gu_own, gu_send, gu_recv, gx_send, gx_recv, gz_send, gz_recv, act, down, ret, ret_recv,
-    load_sem, o_sem, l_sem, zh_sem, ag_sem, y_sem, z_sem, d_sem, gs_sem, g_sem, gz_sem, act_sem, r_sem,
+    load_sem, o_sem, l_sem, zh_sem, ag_sem, w_sem, z_sem, d_sem, gs_sem, g_sem, gz_sem, act_sem, r_sem,
 ):
     me_c = lax.axis_index("ctx")
     me_g = lax.axis_index("grp")
@@ -67,7 +68,7 @@
         (w_uk_hbm, w_uk),
         (qr_hbm, qr),
         (w_uv_hbm, w_uv),
-        (w_out_hbm, w_out),
+        (w_out_hbm, w_out.at[y]),
         (wg_hbm, wgu.at[pl.ds(0, COLS), pl.ds(0, FF)]),
         (wu_hbm, wgu.at[pl.ds(0, COLS), pl.ds(FF, FF)]),
         (wd_hbm, wd),
@@ -77,9 +78,17 @@
         load.start()
     barrier = pltpu.get_barrier_semaphore()
     sibling = near(0, 1 - core)
+
+    def across(dx, dy):
+        return {
+            "ctx": z * NY + (y + dy) % NY,
+            "grp": ((x + dx) % NX) * 4 + zh * 2 + core,
+        }
+
     others = [((z + dz) % NZ) * NY + (y + dy) % NY for dz, dy in OFFSETS]
     sources = [((z + NZ - dz) % NZ) * NY + (y + NY - dy) % NY for dz, dy in OFFSETS]
     greeted = [partner] + [{"ctx": c} for c in others]
+    greeted += [across(dx, dy) for dx in (2, 1, 3) for dy in (2, 1, 3)]
     greeted += [near(d, c) for d in FAR_FIRST[:3] for c in range(2)] + [sibling]
     for device in greeted:
         pl.semaphore_signal(barrier, inc=1, device_id=device, device_id_type=MESH)
@@ -117,11 +126,25 @@
     q_wide[...] = qn[...].astype(F32)
     for load in loads[2:5]:
         load.wait()
+    given = lax.broadcasted_iota(jnp.int32, (ROWS, ROWS), 0)
+    wanted = lax.broadcasted_iota(jnp.int32, (ROWS, ROWS), 1)
+    wanted = (
+        (wanted % ROWS_Y) // ROW_DEV * (NY * ROW_DEV)
+        + wanted // ROWS_Y * ROW_DEV
+        + wanted % ROW_DEV
+    )
+    order = jnp.where(given == wanted, 1.0, 0.0).astype(BF16)
+    rotated = dot(qr[...].reshape(HEADS * ROPE, ROWS), order, 1, 0).astype(BF16)
     for load in loads[5:9]:
         load.start()
     for h in range(HEADS):
-        q = q_wide[pl.ds(h, ROWS, stride=HEADS), :].astype(BF16)
-        queries = jnp.concatenate([dot(w_uk[h], q, 0, 1).astype(BF16), qr[h]], axis=0)
+        q = [
+            q_wide[pl.ds((zz * NY + yy) * ROW_DEV * HEADS + h, ROW_DEV, stride=HEADS), :]
+            for yy in range(NY)
+            for zz in range(NZ)
+        ]
+        q = jnp.concatenate(q, axis=0).astype(BF16)
+        queries = jnp.concatenate([dot(w_uk[h], q, 0, 1).astype(BF16), rotated[h * ROPE : (h + 1) * ROPE]], axis=0)
         s = dot(keys[...], queries, 1, 0) * scale
         top = jnp.max(s, axis=0, keepdims=True)
         raised = jnp.exp(s - top)
@@ -153,7 +176,7 @@
     perm_t[...] = jnp.where(place_of(place) == slot, 1.0, 0.0).astype(BF16)
     res_pad[...] = jnp.zeros((ROW_DEV, PAD), F32)
     res_pad[:, 0:COLS] = residual[...].astype(F32)
-    proj[:, PAD - LANES : PAD] = jnp.zeros((ROWS, LANES), F32)
+    proj[:, PAD - LANES : PAD] = jnp.zeros((ROWS_Y, LANES), F32)
     down[:, PAD - LANES : PAD] = jnp.zeros((SLOTS, LANES), F32)
 
     lane = lax.broadcasted_iota(jnp.int32, (ROW_DEV, PAD), 1)
@@ -178,7 +201,8 @@
     )
 
     loads[5].wait()
-    w_out_t[...] = w_out[...].T
+    for d in (2, 1, 3):
+        send(w_out.at[y], w_out.at[y], w_sem, d, d, {"ctx": z * NY + (y + d) % NY})
 
     for d in FAR_FIRST:
         for c in range(2) if d else (1 - core,):
@@ -205,27 +229,42 @@
     send(zl_send, zl_recv, zh_sem, 1, 1, partner)
     loads[8].wait()
     wd_t[...] = wd[...].T
+    for d in (1, 3, 2):
+        arrive(w_out.at[(y + NY - d) % NY], w_sem, d)
+    for yy in range(NY):
+        turned = w_out[yy].T
+        for xx in range(NX):
+            for c in range(2):
+                for half in range(2):
+                    first = (xx * 2 + c) * 64 + half * 32
+                    w_out_t[half, c, yy, xx] = turned[first : first + 32]
     arrive(zh_recv, zh_sem, 0)
     arrive(zl_recv, zh_sem, 1)
     o, _ = merge([zh_send[...], zh_recv[...]], [l, zl_recv[0:1, :]])
-    att[me_q] = o.astype(BF16)
-    spread(att, ag_sem)
-
-    proj[:, 0:COLS] = dot(att[...].reshape(HEADS * VDIM, ROWS), w_out_t[...], 0, 0)
-    for to in range(NY):
-        parts = []
-        for q in range(QS):
-            part = proj[:, q * LANES : (q + 1) * LANES].reshape(NZ, NY, ROW_DEV, LANES)
-            parts.append(part[:, to])
-        pbuf[to] = jnp.stack(parts, axis=1).reshape(NZ * QS * ROW_DEV, LANES).astype(BF16)
-    for d in (2, 1, 3):
-        to = (y + d) % NY
-        send(pbuf.at[to], p_recv.at[d], y_sem, d, d, {"ctx": z * NY + to})
-    total = pbuf[y].astype(F32)
-    for d in (1, 3, 2):
-        arrive(p_recv.at[d], y_sem, d)
-        total = total + p_recv[d].astype(F32)
-    zbuf[...] = total.reshape(NZ, QS * ROW_DEV, LANES).astype(BF16)
+    left = lax.broadcasted_iota(jnp.int32, (32, LANES), 1) < 64
+    for t in range(2):
+        a, b = o[0:32, t * LANES : (t + 1) * LANES], o[32:64, t * LANES : (t + 1) * LANES]
+        att_send[2 * t] = jnp.where(left, a, pltpu.roll(b, 64, 1)).astype(BF16)
+        att_send[2 * t + 1] = jnp.where(left, pltpu.roll(a, 64, 1), b).astype(BF16)
+    steps = [(dx, dy) for dx in FAR_FIRST for dy in FAR_FIRST][:-1]
+    for n, (dx, dy) in enumerate(steps):
+        send(att_send.at[(y + dy) % NY], att.at[core, y, x], ag_sem, n, n, across(dx, dy))
+    att[core, y, x] = att_send[y]
+    for n, (dx, dy) in enumerate(steps):
+        arrive(att.at[core, (y + NY - dy) % NY, (x + NX - dx) % NX], ag_sem, n)
+    send(att.at[core], att.at[core], ag_sem, len(steps), len(steps), sibling)
+    arrive(att.at[1 - core], ag_sem, len(steps))
+
+    depth = 2 * NY * NX * 32
+    packed = att[...].reshape(depth, LANES)
+    proj[:, 0:COLS] = (
+        dot(packed, w_out_t[0].reshape(depth, COLS), 0, 0)[0:ROWS_Y]
+        + dot(packed, w_out_t[1].reshape(depth, COLS), 0, 0)[ROWS_Y : 2 * ROWS_Y]
+    )
+    parts = [
+        proj[:, q * LANES : (q + 1) * LANES].reshape(NZ, ROW_DEV, LANES) for q in range(QS)
+    ]
+    zbuf[...] = jnp.stack(parts, axis=1).reshape(NZ, QS * ROW_DEV, LANES).astype(BF16)
     for d in (4, 3, 5, 2, 6, 1, 7):
         to = (z + d) % NZ
         send(zbuf.at[to], z_recv.at[d], z_sem, d, d, {"ctx": to * NY + y})
@@ -317,8 +356,8 @@
         ((HEADS, LAT, VDIM), BF16),
         ((LAT + ROPE, KEYS), BF16),
         ((KEYS, LAT + ROPE), BF16),
-        ((COLS, HEADS * VDIM), BF16),
-        ((HEADS * VDIM, COLS), BF16),
+        ((NY, COLS, HEADS * VDIM), BF16),
+        ((2, 2, NY, NX, 32, COLS), BF16),
         ((PAD, 2 * FF), BF16),
         ((COLS, FF), BF16),
         ((FF, COLS), BF16),
@@ -332,10 +371,9 @@
         ((half, ROWS), BF16),
         ((8, ROWS), F32),
         ((8, ROWS), F32),
-        ((near, half, ROWS), BF16),
-        ((ROWS, PAD), F32),
-        ((NY, ROWS, LANES), BF16),
-        ((NY, ROWS, LANES), BF16),
+        ((NY, 32, LANES), BF16),
+        ((2, NY, NX, 32, LANES), BF16),
+        ((ROWS_Y, PAD), F32),
         ((NZ, QS * ROW_DEV, LANES), BF16),
         ((NZ, QS * ROW_DEV, LANES), BF16),
         ((ROW_DEV, PAD), F32),
@@ -353,7 +391,7 @@
         ((NCTX, QS * CAP, LANES), BF16),
         ((NCTX, QS * CAP, LANES), BF16),
     ]
-    sems = [(9,)] + [(2, n) for n in (near, near, 2, near, NY, NZ, NCTX, NX, NX, 1, near, NCTX)]
+    sems = [(9,)] + [(2, n) for n in (near, near, 2, NX * NY, NY, NZ, NCTX, NX, NX, 1, near, NCTX)]
     return pl.pallas_call(
         kernel,
         out_shape=pltpu.VMEM((ROW_DEV, COLS), BF16),

time: 88.9 us -> 99.4 us (1.12)
  Pallas kernels: 88.1 us -> 98.6 us
    pallas_call x1, Pallas kernels: 88.1 us -> 98.6 us  [per_device(): pl.pallas_call(kernel, out_shape=pltpu.VMEM((ROW_DEV, COLS), BF16), in_sp...]
where the time goes in v5:
time: 99.4 us; the launch traced here: 99.2 us
  Pallas kernels  98.6 us (99%)
    pallas_call x1, Pallas kernels, per_device(): pl.pallas_call(kernel, out_shape=pltpu.VMEM((ROW_DEV, COLS), BF16), in_sp...  98.6 us

profile of v5, /device:TPU:1, one launch (start us, length us, event | category | flops | bytes accessed | tf_op | source)
XLA Modules:
  0.0 99.2 jit_solution(9476139942265403674)
XLA Ops:
  0.0 98.6 %layer.1 = bf16[8,448]{1,0:T(8,128)(2,1)S(1)} custom-call(bf16[8,448]{1,0:T(8,128)(2,1)} %residual.1, s32[8,8]{1,0:T(8,128)} %routes.1, f32[8,8]{1,0:T(8,128)} %scores.1, bf16[1024,128]{1,0:T(8,128)(2,1)} %bitcast.14, bf16[4,64,256]{2,1,0:T(8,128)(2,1)} %bitcast.15, bf16[4,128,512]{2,1,0:T(8,128)(2,1)} %w_uk_hbm.1, bf16[4,512,128]{2,1,0:T(8,128)(2,1)} %w_uv_hbm.1, ...), custom_call_target="tpu_custom_call" | custom-call | tf_op jit(solution)/shard_map/layer/pallas_call | solution.py:395
  98.6 0.6 copy.14

commit v6 on v4

--- a/solution.py
+++ b/solution.py
@@ -20,6 +20,7 @@
 PAD = 512
 QS = PAD // LANES
 ROW_DEV = 8
+HALF_Z = 4
 NZ, NY, NX = 8, 4, 4
 NCTX = NZ * NY
 SLOTS = NCTX * CAP
@@ -41,9 +42,10 @@
 
 
 def kernel(
-    residual, routes, scores,
+    residual_hbm, routes_hbm, scores_hbm,
     qn_hbm, qr_hbm, w_uk_hbm, w_uv_hbm, prompt_hbm, w_out_hbm, wg_hbm, wu_hbm, wd_hbm,
     out,
+    residual, routes, scores,
     qn, q_wide, qr, w_uk, w_uv, prompt, keys,
     w_out, w_out_t, wgu, wd, wd_t, perm, perm_t,
     obuf, lse, o_recv, l_recv, zh_send, zh_recv, zl_send, zl_recv, att,
@@ -61,6 +63,14 @@
     def near(d, c):
         return {"grp": ((x + d) % NX) * 4 + zh * 2 + c}
 
+    barrier = pltpu.get_barrier_semaphore()
+    sibling = near(0, 1 - core)
+    others = [((z + dz) % NZ) * NY + (y + dy) % NY for dz, dy in OFFSETS]
+    sources = [((z + NZ - dz) % NZ) * NY + (y + NY - dy) % NY for dz, dy in OFFSETS]
+    greeted = [partner] + [{"ctx": c} for c in others]
+    greeted += [near(d, c) for d in FAR_FIRST[:3] for c in range(2)] + [sibling]
+    for device in greeted:
+        pl.semaphore_signal(barrier, inc=1, device_id=device, device_id_type=MESH)
     pairs = (
         (prompt_hbm, prompt),
         (qn_hbm, qn),
@@ -71,18 +81,13 @@
         (wg_hbm, wgu.at[pl.ds(0, COLS), pl.ds(0, FF)]),
         (wu_hbm, wgu.at[pl.ds(0, COLS), pl.ds(FF, FF)]),
         (wd_hbm, wd),
+        (residual_hbm, residual),
+        (routes_hbm, routes),
+        (scores_hbm, scores),
     )
     loads = [pltpu.make_async_copy(a, b, load_sem.at[i]) for i, (a, b) in enumerate(pairs)]
     for load in loads[0:5]:
         load.start()
-    barrier = pltpu.get_barrier_semaphore()
-    sibling = near(0, 1 - core)
-    others = [((z + dz) % NZ) * NY + (y + dy) % NY for dz, dy in OFFSETS]
-    sources = [((z + NZ - dz) % NZ) * NY + (y + NY - dy) % NY for dz, dy in OFFSETS]
-    greeted = [partner] + [{"ctx": c} for c in others]
-    greeted += [near(d, c) for d in FAR_FIRST[:3] for c in range(2)] + [sibling]
-    for device in greeted:
-        pl.semaphore_signal(barrier, inc=1, device_id=device, device_id_type=MESH)
     sent = []
 
     def send(src, dst, sems, n, at, device):
@@ -99,7 +104,7 @@
             device_id=partner, device_id_type=MESH,
         ).wait_recv()
 
-    def spread(buf, sems):
+    def spread(buf, sems, use=lambda total, q: total, total=0):
         for d in (2, 1, 3):
             send(buf.at[me_q], buf.at[me_q], sems, d, d, near(d, core))
         send(buf.at[me_q], buf.at[me_q], sems, NX, NX, sibling)
@@ -108,7 +113,18 @@
             arrive(buf.at[got], sems, d)
             send(buf.at[got], buf.at[got], sems, NX + d, NX + d, sibling)
         for d in (0, 1, 3, 2):
-            arrive(buf.at[((x + NX - d) % NX) * 2 + 1 - core], sems, NX + d)
+            total = use(total, ((x + NX - d) % NX) * 2 + core)
+        for d in (0, 1, 3, 2):
+            got = ((x + NX - d) % NX) * 2 + 1 - core
+            arrive(buf.at[got], sems, NX + d)
+            total = use(total, got)
+        return total
+
+    def fold(v):
+        return jnp.concatenate([v[:, 0:LANES], v[:, LANES:ROWS]] * 4, axis=0)
+
+    def unfold(v):
+        return jnp.concatenate([v[0:1], v[1:2]], axis=1)
 
     scale = (NOPE + ROPE) ** -0.5
     loads[0].wait()
@@ -117,7 +133,7 @@
     q_wide[...] = qn[...].astype(F32)
     for load in loads[2:5]:
         load.wait()
-    for load in loads[5:9]:
+    for load in loads[5:12]:
         load.start()
     for h in range(HEADS):
         q = q_wide[pl.ds(h, ROWS, stride=HEADS), :].astype(BF16)
@@ -131,7 +147,7 @@
         values = dot(w_uv[h], high, 0, 0) + dot(w_uv[h], low, 0, 0)
         o = (values / total).astype(BF16)
         obuf[h] = o.reshape(2, VDIM // 2, ROWS)
-        lse[h] = jnp.broadcast_to(top + jnp.log(total), (8, ROWS))
+        lse[h] = fold(top + jnp.log(total))
     pl.semaphore_wait(barrier, len(greeted))
     for d in FAR_FIRST:
         h = (x + d) % NX
@@ -151,6 +167,8 @@
 
     perm[...] = jnp.where(place_of(slot) == place, 1.0, 0.0).astype(BF16)
     perm_t[...] = jnp.where(place_of(place) == slot, 1.0, 0.0).astype(BF16)
+    for load in loads[9:12]:
+        load.wait()
     res_pad[...] = jnp.zeros((ROW_DEV, PAD), F32)
     res_pad[:, 0:COLS] = residual[...].astype(F32)
     proj[:, PAD - LANES : PAD] = jnp.zeros((ROWS, LANES), F32)
@@ -198,16 +216,16 @@
             o = o + v.astype(F32) * s
         return o / total, top + jnp.log(total)
 
-    o, l = merge([o_recv[i] for i in range(2 * NX)], [l_recv[i, 0:1, :] for i in range(2 * NX)])
+    o, l = merge([o_recv[i] for i in range(2 * NX)], [unfold(l_recv[i]) for i in range(2 * NX)])
     zh_send[...] = o.astype(BF16)
-    zl_send[...] = jnp.broadcast_to(l, (8, ROWS))
+    zl_send[...] = fold(l)
     send(zh_send, zh_recv, zh_sem, 0, 0, partner)
     send(zl_send, zl_recv, zh_sem, 1, 1, partner)
     loads[8].wait()
     wd_t[...] = wd[...].T
     arrive(zh_recv, zh_sem, 0)
     arrive(zl_recv, zh_sem, 1)
-    o, _ = merge([zh_send[...], zh_recv[...]], [l, zl_recv[0:1, :]])
+    o, _ = merge([zh_send[...], zh_recv[...]], [l, unfold(zl_recv[...])])
     att[me_q] = o.astype(BF16)
     spread(att, ag_sem)
 
@@ -217,21 +235,28 @@
         for q in range(QS):
             part = proj[:, q * LANES : (q + 1) * LANES].reshape(NZ, NY, ROW_DEV, LANES)
             parts.append(part[:, to])
-        pbuf[to] = jnp.stack(parts, axis=1).reshape(NZ * QS * ROW_DEV, LANES).astype(BF16)
-    for d in (2, 1, 3):
-        to = (y + d) % NY
-        send(pbuf.at[to], p_recv.at[d], y_sem, d, d, {"ctx": z * NY + to})
-    total = pbuf[y].astype(F32)
-    for d in (1, 3, 2):
-        arrive(p_recv.at[d], y_sem, d)
-        total = total + p_recv[d].astype(F32)
-    zbuf[...] = total.reshape(NZ, QS * ROW_DEV, LANES).astype(BF16)
-    for d in (4, 3, 5, 2, 6, 1, 7):
-        to = (z + d) % NZ
-        send(zbuf.at[to], z_recv.at[d], z_sem, d, d, {"ctx": to * NY + y})
+        block = jnp.stack(parts, axis=1).reshape(2, HALF_Z * QS * ROW_DEV, LANES)
+        pbuf[to] = block.astype(BF16)
+    halves = (1 - z // HALF_Z, z // HALF_Z)
+    for k, half in enumerate(halves):
+        for d in (2, 1, 3):
+            to = (y + d) % NY
+            device = {"ctx": z * NY + to}
+            send(pbuf.at[to, half], p_recv.at[d, k], y_sem, d * 2 + k, d * 2 + k, device)
+    for k, half in enumerate(halves):
+        total = pbuf[y, half].astype(F32)
+        for d in (1, 3, 2):
+            arrive(p_recv.at[d, k], y_sem, d * 2 + k)
+            total = total + p_recv[d, k].astype(F32)
+        zbuf[half] = total.reshape(HALF_Z, QS * ROW_DEV, LANES).astype(BF16)
+        for j in range(HALF_Z)[k:]:
+            at = (z + j) % HALF_Z
+            device = {"ctx": (half * HALF_Z + at) * NY + y}
+            n = j + HALF_Z * (1 - k)
+            send(zbuf.at[half, at], z_recv.at[n], z_sem, n, n, device)
     hidden = jnp.concatenate([res_pad[:, q * LANES : (q + 1) * LANES] for q in range(QS)], axis=0)
-    hidden = hidden + zbuf[z].astype(F32)
-    for d in (1, 7, 2, 6, 3, 5, 4):
+    hidden = hidden + zbuf[halves[1], z % HALF_Z].astype(F32)
+    for d in range(1, NZ):
         arrive(z_recv.at[d], z_sem, d)
         hidden = hidden + z_recv[d].astype(F32)
 
@@ -278,9 +303,12 @@
     sums = sums + gz_recv[...].astype(F32)
     gate, up = sums[0:SLOTS], sums[SLOTS : 2 * SLOTS]
     act[me_q] = (gate / (1.0 + jnp.exp(-gate)) * up).astype(BF16)
-    spread(act, act_sem)
-    hidden_units = jnp.concatenate([act[q] for q in range(2 * NX)], axis=1)
-    down[:, 0:COLS] = dot(hidden_units, wd_t[...], 1, 0)
+    def add(total, q):
+        rows_q = pl.ds(pl.multiple_of(q * LANES, LANES), LANES)
+        return total + dot(act[q], wd_t[rows_q, :], 1, 0)
+
+    total = spread(act, act_sem, add, jnp.zeros((SLOTS, COLS), F32))
+    down[:, 0:COLS] = total
 
     result = jnp.concatenate([down[:, q * LANES : (q + 1) * LANES] for q in range(QS)], axis=0)
     packed = dot(perm_t[...], result.astype(BF16), 1, 0).astype(BF16)
@@ -310,6 +338,9 @@
     near = 2 * NX
     half = VDIM // 2
     scratch = [
+        ((ROW_DEV, COLS), BF16),
+        ((ROW_DEV, TOPK), jnp.int32),
+        ((ROW_DEV, TOPK), F32),
         ((ROWS * HEADS, NOPE), BF16),
         ((ROWS * HEADS, NOPE), F32),
         ((HEADS, ROPE, ROWS), BF16),
@@ -325,18 +356,18 @@
         ((PAD, PAD), BF16),
         ((PAD, PAD), BF16),
         ((HEADS, 2, half, ROWS), BF16),
-        ((HEADS, 8, ROWS), F32),
+        ((HEADS, 8, LANES), F32),
         ((near, half, ROWS), BF16),
-        ((near, 8, ROWS), F32),
+        ((near, 8, LANES), F32),
         ((half, ROWS), BF16),
         ((half, ROWS), BF16),
-        ((8, ROWS), F32),
-        ((8, ROWS), F32),
+        ((8, LANES), F32),
+        ((8, LANES), F32),
         ((near, half, ROWS), BF16),
         ((ROWS, PAD), F32),
-        ((NY, ROWS, LANES), BF16),
-        ((NY, ROWS, LANES), BF16),
-        ((NZ, QS * ROW_DEV, LANES), BF16),
+        ((NY, 2, ROWS // 2, LANES), BF16),
+        ((NY, 2, ROWS // 2, LANES), BF16),
+        ((2, HALF_Z, QS * ROW_DEV, LANES), BF16),
         ((NZ, QS * ROW_DEV, LANES), BF16),
         ((ROW_DEV, PAD), F32),
         ((NCTX, QS * CAP, LANES), BF16),
@@ -353,11 +384,11 @@
         ((NCTX, QS * CAP, LANES), BF16),
         ((NCTX, QS * CAP, LANES), BF16),
     ]
-    sems = [(9,)] + [(2, n) for n in (near, near, 2, near, NY, NZ, NCTX, NX, NX, 1, near, NCTX)]
+    sems = [(12,)] + [(2, n) for n in (near, near, 2, near, 2 * NY, NZ, NCTX, NX, NX, 1, near, NCTX)]
     return pl.pallas_call(
         kernel,
         out_shape=pltpu.VMEM((ROW_DEV, COLS), BF16),
-        in_specs=[vmem] * 3 + [hbm] * 9,
+        in_specs=[hbm] * 12,
         out_specs=vmem,
         scratch_shapes=[pltpu.VMEM(*s) for s in scratch] + [dma(s) for s in sems],
         compiler_params=pltpu.CompilerParams(

time: 88.9 us -> 88.1 us (level)
  no operation moved by 1% of the time
where the time goes in v6:
time: 88.1 us; the launch traced here: 87.9 us
  Pallas kernels  87.3 us (99%)
    pallas_call x1, Pallas kernels, per_device(): pl.pallas_call(kernel, out_shape=pltpu.VMEM((ROW_DEV, COLS), BF16), in_sp...  87.3 us

profile of v6, /device:TPU:1, one launch (start us, length us, event | category | flops | bytes accessed | tf_op | source)
XLA Modules:
  0.0 87.9 jit_solution(5771054630023383537)
XLA Ops:
  0.0 87.3 %layer.1 = bf16[8,448]{1,0:T(8,128)(2,1)S(1)} custom-call(bf16[8,448]{1,0:T(8,128)(2,1)} %residual_hbm.1, s32[8,8]{1,0:T(8,128)} %routes_hbm.1, f32[8,8]{1,0:T(8,128)} %scores_hbm.1, bf16[1024,128]{1,0:T(8,128)(2,1)} %bitcast.14, bf16[4,64,256]{2,1,0:T(8,128)(2,1)} %bitcast.15, bf16[4,128,512]{2,1,0:T(8,128)(2,1)} %w_uk_hbm.1, ...), custom_call_target="tpu_custom_call" | custom-call | tf_op jit(solution)/shard_map/layer/pallas_call | solution.py:388
  87.3 0.6 copy.14

commit v7 on v6

--- a/solution.py
+++ b/solution.py
@@ -50,7 +50,7 @@
     w_out, w_out_t, wgu, wd, wd_t, perm, perm_t,
     obuf, lse, o_recv, l_recv, zh_send, zh_recv, zl_send, zl_recv, att,
     proj, pbuf, p_recv, zbuf, z_recv, res_pad, disp, arrived,
-    gu_own, gu_send, gu_recv, gx_send, gx_recv, gz_send, gz_recv, act, down, ret, ret_recv,
+    gu_own, gu_send, gu_recv, gx_send, gx_recv, gz_send, gz_recv, act, down, ret, ret_recv, parts_high, parts_low,
     load_sem, o_sem, l_sem, zh_sem, ag_sem, y_sem, z_sem, d_sem, gs_sem, g_sem, gz_sem, act_sem, r_sem,
 ):
     me_c = lax.axis_index("ctx")
@@ -195,6 +195,9 @@
         [jnp.where(block_of == q, picked * weight, 0.0) for q in range(QS)], axis=0
     )
 
+    for zz in range(NZ):
+        some = pick_weight[:, zz * NY * QS * CAP : (zz + 1) * NY * QS * CAP]
+        parts_high[zz], parts_low[zz] = split(some)
     loads[5].wait()
     w_out_t[...] = w_out[...].T
 
@@ -314,10 +317,13 @@
     packed = dot(perm_t[...], result.astype(BF16), 1, 0).astype(BF16)
     ret[...] = packed.reshape(NCTX, QS * CAP, LANES)
     to_all(ret, ret_recv, r_sem)
-    from_all(ret_recv, r_sem)
-    returned = ret_recv[...].reshape(PAD, LANES)
-    high, low = split(pick_weight)
-    final = (hidden + dot(high, returned, 1, 0) + dot(low, returned, 1, 0)).astype(BF16)
+    for g in range(NZ):
+        for n in range(g * NY, min(g * NY + NY, len(sources))):
+            arrive(ret_recv.at[sources[n]], r_sem, n)
+        at = (z + NZ - OFFSETS[g * NY][0]) % NZ
+        group = ret_recv[pl.ds(at * NY, NY)].reshape(NY * QS * CAP, LANES)
+        hidden = hidden + dot(parts_high[at], group, 1, 0) + dot(parts_low[at], group, 1, 0)
+    final = hidden.astype(BF16)
     for q in range(QS):
         width = min(LANES, COLS - q * LANES)
         out[:, q * LANES : q * LANES + width] = final[q * ROW_DEV : (q + 1) * ROW_DEV, 0:width]
@@ -383,6 +389,8 @@
         ((SLOTS, PAD), F32),
         ((NCTX, QS * CAP, LANES), BF16),
         ((NCTX, QS * CAP, LANES), BF16),
+        ((NZ, QS * ROW_DEV, NY * QS * CAP), BF16),
+        ((NZ, QS * ROW_DEV, NY * QS * CAP), BF16),
     ]
     sems = [(12,)] + [(2, n) for n in (near, near, 2, near, 2 * NY, NZ, NCTX, NX, NX, 1, near, NCTX)]
     return pl.pallas_call(

time: 88.1 us -> 88.1 us (level)
  no operation moved by 1% of the time
where the time goes in v7:
time: 88.1 us; the launch traced here: 87.9 us
  Pallas kernels  87.3 us (99%)
    pallas_call x1, Pallas kernels, per_device(): pl.pallas_call(kernel, out_shape=pltpu.VMEM((ROW_DEV, COLS), BF16), in_sp...  87.3 us

profile of v7, /device:TPU:1, one launch (start us, length us, event | category | flops | bytes accessed | tf_op | source)
XLA Modules:
  0.0 87.9 jit_solution(3072297828929589996)
XLA Ops:
  0.0 87.3 %layer.1 = bf16[8,448]{1,0:T(8,128)(2,1)S(1)} custom-call(bf16[8,448]{1,0:T(8,128)(2,1)} %residual_hbm.1, s32[8,8]{1,0:T(8,128)} %routes_hbm.1, f32[8,8]{1,0:T(8,128)} %scores_hbm.1, bf16[1024,128]{1,0:T(8,128)(2,1)} %bitcast.14, bf16[4,64,256]{2,1,0:T(8,128)(2,1)} %bitcast.15, bf16[4,128,512]{2,1,0:T(8,128)(2,1)} %w_uk_hbm.1, ...), custom_call_target="tpu_custom_call" | custom-call | tf_op jit(solution)/shard_map/layer/pallas_call | solution.py:396
  87.3 0.6 copy.14
